TPU v7x, 32 devices: a whole 2x2x4 slice. The times are simulated.
32 devices in a mesh: grp: 16 (over z, y, x), blk: 2 (over core).
Axes of the slice: x: 2, y: 2, z: 4, core: 2. Of those that a mesh axis runs over, the one named last changes fastest.
Arguments:
- image: bfloat16 [256, 1024], P(('blk', 'grp')), may hold values from -16 to 16
- text: bfloat16 [256, 1024], P(('grp', 'blk')), may hold values from -16 to 16
- mimage: bfloat16 [256, 1024], P(('blk', 'grp')), may hold values from -16 to 16
- mtext: bfloat16 [256, 1024], P(('grp', 'blk')), may hold values from -16 to 16
Outputs:
- grad_image: float32 [256, 1024], P(('blk', 'grp'))
- grad_text: float32 [256, 1024], P(('grp', 'blk'))
- loss: float32 [], replicated
All inputs are finite; a program needn't handle non-finite values.
Results may differ from a plain program's by a relative error of at most 0.0037.
Values may be sent and summed in bfloat16 or wider, within the bound.
A program may use at most 64 MiB of HBM per device.

v0:
```python
import jax
import jax.numpy as jnp
from jax import lax
from jax.sharding import PartitionSpec as P

mix_weight = 0.4
very_low = -1e30


def combined_all(value, axis, join):
    pieces = jax.tree.map(lambda part: lax.all_gather(part, axis), value)
    head = jax.tree.map(lambda part: part[0], pieces)
    tail = jax.tree.map(lambda part: part[1:], pieces)
    running, _ = lax.scan(lambda running, share: (join(running, share), None), head, tail)
    return running


def from_behind(value, axis, steps):
    count = lax.axis_size(axis)
    pairs = [(source, (source + steps) % count) for source in range(count)]
    return lax.ppermute(value, axis, pairs)


def logits_of(left_rows, right_rows):
    scale_factor = left_rows.shape[1] ** (-0.5)
    product = lax.dot_general(
        left_rows, right_rows, (((1,), (1,)), ((), ())), preferred_element_type=jnp.float32
    )
    return product * scale_factor


def fold_stats(run_max, run_total, scores, along):
    new_max = jnp.maximum(run_max, jnp.max(scores, axis=along))
    spread = jnp.exp(scores - jnp.expand_dims(new_max, along))
    new_total = run_total * jnp.exp(run_max - new_max) + jnp.sum(spread, axis=along)
    return (new_max, new_total)


def join_pair(max_a, total_a, max_b, total_b):
    top_max = jnp.maximum(max_a, max_b)
    return (top_max, total_a * jnp.exp(max_a - top_max) + total_b * jnp.exp(max_b - top_max))


def join_stats(earlier, later):
    on_max, on_total = join_pair(earlier[0], earlier[1], later[0], later[1])
    mom_max, mom_total = join_pair(earlier[2], earlier[3], later[2], later[3])
    return (on_max, on_total, mom_max, mom_total)


def merge_rows(row_stats):
    merged = combined_all(row_stats, "grp", join_stats)
    return (merged[0] + jnp.log(merged[1]), merged[2] + jnp.log(merged[3]))


def gradient_tile(
    score_on, score_mom, diagonal, row_online, row_momentum, col_online, col_momentum
):
    prob_row = jnp.exp(score_on - row_online[None, :])
    prob_col = jnp.exp(score_on - col_online[:, None])
    target_row = (
        mix_weight * jnp.exp(score_mom - row_momentum[None, :]) + (1.0 - mix_weight) * diagonal
    )
    target_col = (
        mix_weight * jnp.exp(score_mom - col_momentum[:, None]) + (1.0 - mix_weight) * diagonal
    )
    grad_tile = 0.5 * (prob_row - target_row + (prob_col - target_col))
    cross_term = jnp.sum((target_row + target_col) * score_on)
    return (grad_tile.astype(jnp.bfloat16), cross_term)


def local(image, text, mimage, mtext):
    tile_rows = image.shape[0]
    feat_width = image.shape[1]
    group_size = lax.axis_size("grp")
    cycle_size = lax.axis_size("blk")
    group_pos = lax.axis_index("grp")
    cycle_pos = lax.axis_index("blk")
    images, mimages = (
        lax.all_gather(image, "grp", axis=0, tiled=True),
        lax.all_gather(mimage, "grp", axis=0, tiled=True),
    )
    image_span = images.shape[0]
    image_ids = cycle_pos * image_span + lax.iota(jnp.int32, image_span)
    group_base = group_pos * cycle_size * tile_rows
    low_rows = jnp.full((image_span,), very_low, jnp.float32)
    zero_rows = jnp.zeros((image_span,), jnp.float32)
    low_cols = jnp.full((tile_rows,), very_low, jnp.float32)
    zero_cols = jnp.zeros((tile_rows,), jnp.float32)
    kept_init = ()

    def first_turn(turn_index, carry):
        moving_text, moving_stats, row_stats, kept = carry
        own_text, own_mtext = moving_text
        cmax_on, csum_on, cmax_mom, csum_mom = moving_stats
        score_on = logits_of(own_text, images)
        score_mom = logits_of(own_mtext, mimages)
        rmax_on, rsum_on = fold_stats(row_stats[0], row_stats[1], score_on, 0)
        rmax_mom, rsum_mom = fold_stats(row_stats[2], row_stats[3], score_mom, 0)
        cmax_on, csum_on = fold_stats(cmax_on, csum_on, score_on, 1)
        cmax_mom, csum_mom = fold_stats(cmax_mom, csum_mom, score_mom, 1)
        moving_text = from_behind((own_text, own_mtext), "blk", 1)
        moving_stats = from_behind((cmax_on, csum_on, cmax_mom, csum_mom), "blk", 1)
        return (moving_text, moving_stats, (rmax_on, rsum_on, rmax_mom, rsum_mom), kept)

    first_init = (
        (text, mtext),
        (low_cols, zero_cols, low_cols, zero_cols),
        (low_rows, zero_rows, low_rows, zero_rows),
        kept_init,
    )
    unused_text, col_stats, row_stats, kept = lax.fori_loop(0, cycle_size, first_turn, first_init)
    col_online = col_stats[0] + jnp.log(col_stats[1])
    col_momentum = col_stats[2] + jnp.log(col_stats[3])
    row_online, row_momentum = merge_rows(row_stats)

    def second_turn(turn_index, carry):
        moving_text, moving_grad, grad_all, seen_text, cross_sum = carry
        col_on, col_mom, grad_text_acc = moving_grad
        own_text, own_mtext = moving_text
        score_on = logits_of(own_text, images)
        score_mom = logits_of(own_mtext, mimages)
        source_pos = (cycle_pos - turn_index) % cycle_size
        text_ids = group_base + source_pos * tile_rows + lax.iota(jnp.int32, tile_rows)
        diagonal = (text_ids[:, None] == image_ids[None, :]).astype(jnp.float32)
        grad_tile, cross_term = gradient_tile(
            score_on, score_mom, diagonal, row_online, row_momentum, col_on, col_mom
        )
        grad_text_acc = grad_text_acc + jnp.dot(
            grad_tile, images, preferred_element_type=jnp.float32
        )
        grad_all = lax.dynamic_update_slice_in_dim(grad_all, grad_tile, source_pos * tile_rows, 0)
        seen_text = lax.dynamic_update_slice_in_dim(seen_text, own_text, source_pos * tile_rows, 0)
        outgoing = (own_text, own_mtext)
        moving_text = from_behind((outgoing[0], outgoing[1]), "blk", 1)
        moving_grad = from_behind((col_on, col_mom, grad_text_acc), "blk", 1)
        return (moving_text, moving_grad, grad_all, seen_text, cross_sum + cross_term)

    text_init = (text, mtext)
    second_init = (
        text_init,
        (col_online, col_momentum, jnp.zeros((tile_rows, feat_width), jnp.float32)),
        jnp.zeros((cycle_size * tile_rows, image_span), jnp.bfloat16),
        jnp.zeros((cycle_size * tile_rows, feat_width), jnp.bfloat16),
        jnp.zeros((), jnp.float32),
    )
    final_carry = lax.fori_loop(0, cycle_size, second_turn, second_init)
    grad_text = final_carry[1][2]
    grad_all = final_carry[2]
    seen_text = final_carry[3]
    cross_sum = final_carry[4]
    image_part = lax.dot_general(
        grad_all, seen_text, (((0,), (0,)), ((), ())), preferred_element_type=jnp.float32
    )
    grad_image = lax.psum_scatter(image_part, "grp", scatter_dimension=0, tiled=True)
    own_rows = lax.dynamic_slice_in_dim(row_online, group_pos * tile_rows, tile_rows, 0)
    local_loss = jnp.sum(own_rows) + jnp.sum(col_online) - cross_sum
    total_pairs = tile_rows * group_size * cycle_size
    loss = lax.psum(local_loss, ("grp", "blk")) / (2.0 * total_pairs)
    return (grad_image, grad_text, loss)


def solution(mesh):
    in_specs = (
        P(("blk", "grp"), None),
        P(("grp", "blk"), None),
        P(("blk", "grp"), None),
        P(("grp", "blk"), None),
    )
    out_specs = (P(("blk", "grp"), None), P(("grp", "blk"), None), P())
    return jax.shard_map(local, mesh=mesh, in_specs=in_specs, out_specs=out_specs, check_vma=False)
```

profile of v0, /device:TPU:0, one launch (start us, length us, event | category | flops | bytes accessed | tf_op | source)
XLA Modules:
  0.0 340.6 jit_solution(3464465050889982109)
XLA Ops:
  7.2 0.7 copy.101
  8.0 0.6 copy-done
  8.6 0.7 copy-done.10
  9.3 43.9 %all_gather.30 = bf16[128,1024]{1,0:T(8,128)(2,1)S(1)} all-gather(bf16[8,1024]{1,0:T(8,128)(2,1)S(1)} %copy-done.10), channel_id=1, replica_groups=mesh['grp'=16,'blk'=2] {'grp'}, dimensions={0}, use_global_device_ids=true | all-gather | bytes 278528 | tf_op jit(solution)/shard_map/all_gather | solution.py:79
  53.2 37.0 %all_gather.31 = bf16[128,1024]{1,0:T(8,128)(2,1)S(1)} all-gather(bf16[8,1024]{1,0:T(8,128)(2,1)S(1)} %copy-done.11), channel_id=1, replica_groups=mesh['grp'=16,'blk'=2] {'grp'}, dimensions={0}, use_global_device_ids=true | all-gather | bytes 278528 | tf_op jit(solution)/shard_map/all_gather | solution.py:80
  90.2 7.6 %while.77 = (s32[]{:T(128)}, bf16[8,1024]{1,0:T(8,128)(2,1)S(1)}, bf16[8,1024]{1,0:T(8,128)(2,1)S(1)}, f32[8]{0:T(128)S(1)}, f32[8]{0:T(128)S(1)}, /*index=5*/f3...) while((s32[]{:T(128)}, bf16[8,1024]{1,0:T(8,128)(2,1)S(1)}, ...), condition=%wide.region_9.0_spmd.clone, body=%wide.region_0.0_spmd.clone.sunk | while | flops 4209955 | bytes 785097 | solution.py:111
  90.3 0.3 fusion.65
  90.6 0.6 collective-permute-start.9
  91.4 0.5 collective-permute-start.5
  91.9 0.3 fusion.63
  92.6 0.5 collective-permute-start.8
  93.1 0.3 collective-permute-done.7
  93.4 0.5 collective-permute-done.8
  93.9 0.4 collective-permute-start.6
  94.3 0.3 fusion.65
  95.1 0.4 collective-permute-start.10
  95.7 0.3 fusion.63
  96.0 0.4 collective-permute-start.7
  96.6 0.3 collective-permute-start.8
  96.9 0.3 collective-permute-done.7
  97.2 0.6 collective-permute-done.8
  97.8 37.3 %all-gather.6 = f32[16,1,128]{2,1,0:T(1,128)S(1)} all-gather(f32[1,1,128]{2,1,0:T(1,128)S(1)} %bitcast.84), channel_id=4, replica_groups=mesh['grp'=16,'blk'=2] {'grp'}, dimensions={0}, use_global_device_ids=true | all-gather | bytes 8704 | tf_op jit(solution)/shard_map/all_gather | solution.py:11
  135.1 0.6 copy-done.6
  135.7 35.2 %all-gather.5 = f32[16,1,128]{2,1,0:T(1,128)S(1)} all-gather(f32[1,1,128]{2,1,0:T(1,128)S(1)} %bitcast.87), channel_id=3, replica_groups=mesh['grp'=16,'blk'=2] {'grp'}, dimensions={0}, use_global_device_ids=true | all-gather | bytes 8704 | tf_op jit(solution)/shard_map/all_gather | solution.py:11
  170.9 0.6 copy-done.7
  171.5 37.3 %all-gather.7 = f32[16,1,128]{2,1,0:T(1,128)S(1)} all-gather(f32[1,1,128]{2,1,0:T(1,128)S(1)} %bitcast.86), channel_id=5, replica_groups=mesh['grp'=16,'blk'=2] {'grp'}, dimensions={0}, use_global_device_ids=true | all-gather | bytes 8704 | tf_op jit(solution)/shard_map/all_gather | solution.py:11
  208.8 0.6 copy-done.8
  209.4 35.2 %all-gather.4 = f32[16,1,128]{2,1,0:T(1,128)S(1)} all-gather(f32[1,1,128]{2,1,0:T(1,128)S(1)} %bitcast.85), channel_id=2, replica_groups=mesh['grp'=16,'blk'=2] {'grp'}, dimensions={0}, use_global_device_ids=true | all-gather | bytes 8704 | tf_op jit(solution)/shard_map/all_gather | solution.py:11
  244.6 0.6 copy-done.9
  245.3 0.7 slice-done.1
  246.0 0.7 slice-done.2
  246.7 0.7 slice-done.3
  247.4 0.7 while.75
  248.1 0.6 fusion.22
  248.8 0.7 copy-done.1
  249.5 6.5 %while.76 = (s32[]{:T(128)}, bf16[8,1024]{1,0:T(8,128)(2,1)S(1)}, bf16[8,1024]{1,0:T(8,128)(2,1)S(1)}, f32[8]{0:T(128)S(1)}, f32[8]{0:T(128)S(1)}, /*index=5*/f3...) while((s32[]{:T(128)}, bf16[8,1024]{1,0:T(8,128)(2,1)S(1)}, ...), condition=%wide.region_14.15_spmd.clone, body=%wide.region_12.14_spmd.clone.sunk | while | flops 6328475 | bytes 1277496 | solution.py:146
  249.5 0.5 collective-permute-start.3
  250.1 0.4 collective-permute-start
  251.2 0.7 multiply_reduce_fusion.2
  252.6 0.5 collective-permute-start.2
  253.2 0.4 collective-permute-start.1
  254.2 0.4 collective-permute-start.4
  254.7 0.7 multiply_reduce_fusion.2
  256.0 1.1 fusion.23
  257.1 0.7 dynamic-slice_reduce_fusion
  259.1 37.2 %psum.7 = f32[]{:T(128)} all-reduce(f32[]{:T(128)S(6)} %sub.193), channel_id=1, replica_groups=mesh['grp'=16,'blk'=2] {'grp','blk'}, use_global_device_ids=true, to_apply=%region_18.19 | all-reduce | flops 1 | bytes 8 | tf_op jit(solution)/shard_map/psum | solution.py:158
  297.0 35.0 %reduce-scatter.2.cloned.1.call-done = f32[8,1024]{1,0:T(8,128)} async-done(((f32[128,1024]{1,0:T(8,128)}), f32[8,1024]{1,0:T(8,128)}) %reduce-scatter.2.cloned.1.call-update) | async-done | bytes 32784 | tf_op jit(solution)/shard_map/reduce_scatter | solution.py:154
  332.0 0.6 copy.104
  (140 shorter events, 3.9 us)
Async XLA Ops:
  7.2 0.8 copy-start.12
  7.2 324.8 %reduce-scatter.2.cloned.1.call-start = ((), (), s32[]{:S(2)}) async-start(), calls=%async_computation.1 | async-start | bytes 557056 | tf_op jit(solution)/shard_map/reduce_scatter | solution.py:154
  7.9 0.6 copy-start
  7.9 0.6 copy-start.3
  8.6 0.7 copy-start.10
  9.3 43.9 %copy-start.11 = (bf16[8,1024]{1,0:T(8,128)(2,1)S(1)}, bf16[8,1024]{1,0:T(8,128)(2,1)}, u32[]{:S(2)}) copy-start(bf16[8,1024]{1,0:T(8,128)(2,1)} %param.12) | copy-start | bytes 49156
  53.2 37.0 %copy-start.2 = (bf16[8,1024]{1,0:T(8,128)(2,1)S(1)}, bf16[8,1024]{1,0:T(8,128)(2,1)}, u32[]{:S(2)}) copy-start(bf16[8,1024]{1,0:T(8,128)(2,1)} %copy-done) | copy-start | bytes 49156
  53.2 37.0 %copy-start.5 = (bf16[8,1024]{1,0:T(8,128)(2,1)S(1)}, bf16[8,1024]{1,0:T(8,128)(2,1)}, u32[]{:S(2)}) copy-start(bf16[8,1024]{1,0:T(8,128)(2,1)} %copy-done.3) | copy-start | bytes 49156
  90.2 3.8 %collective-permute-start.6 = (bf16[8,1024]{1,0:T(8,128)(2,1)S(1)}, bf16[8,1024]{1,0:T(8,128)(2,1)S(1)}, u32[]{:S(2)}, u32[]{:S(2)}) collective-permute-start(bf16[8,1024]{1,0:T(8,128)(2,1)S(1)} %copy.34), channel_id=1, source_target_pairs={{0,1},{1,0},{2,3},{3,2},{4,5},{5,4},{6,7},{7,6},{8,9},{9,8},{10,11... | collective-permute-start | bytes 49160 | tf_op jit(solution)/shard_map/while/body/eval_jaxpr/ppermute | solution.py:21
  90.6 2.0 collective-permute-start.9
  91.3 2.1 collective-permute-start.10
  91.4 2.5 collective-permute-start.5
  92.2 1.2 collective-permute-start.7
  92.6 1.3 collective-permute-start.8
  93.9 3.8 %collective-permute-start.6 = (bf16[8,1024]{1,0:T(8,128)(2,1)S(1)}, bf16[8,1024]{1,0:T(8,128)(2,1)S(1)}, u32[]{:S(2)}, u32[]{:S(2)}) collective-permute-start(bf16[8,1024]{1,0:T(8,128)(2,1)S(1)} %copy.34), channel_id=1, source_target_pairs={{0,1},{1,0},{2,3},{3,2},{4,5},{5,4},{6,7},{7,6},{8,9},{9,8},{10,11... | collective-permute-start | bytes 49160 | tf_op jit(solution)/shard_map/while/body/eval_jaxpr/ppermute | solution.py:21
  94.6 2.0 collective-permute-start.9
  95.1 2.1 collective-permute-start.10
  95.5 2.3 collective-permute-start.5
  96.0 1.2 collective-permute-start.7
  96.6 1.2 collective-permute-start.8
  135.1 0.6 copy-start.6
  170.9 0.6 copy-start.7
  208.8 0.6 copy-start.8
  244.6 0.6 copy-start.9
  244.6 0.7 slice-start
  245.3 0.7 slice-start.1
  246.0 0.7 slice-start.2
  246.7 0.7 slice-start.3
  248.8 0.7 copy-start.1
  248.8 0.7 copy-start.4
  249.5 3.0 collective-permute-start.2
  249.5 3.0 collective-permute-start.3
  250.0 2.5 collective-permute-start.1
  250.1 2.4 collective-permute-start
  251.1 1.5 collective-permute-start.4
  252.6 3.4 %collective-permute-start.2 = (f32[8]{0:T(128)S(1)}, f32[8]{0:T(128)S(1)}, u32[]{:S(2)}, u32[]{:S(2)}) collective-permute-start(f32[8]{0:T(128)S(1)} %copy.81), channel_id=1, source_target_pairs={{0,1},{1,0},{2,3},{3,2},{4,5},{5,4},{6,7},{7,6},{8,9},{9,8},{10,11... | collective-permute-start | bytes 104 | tf_op jit(solution)/shard_map/while/body/eval_jaxpr/ppermute | solution.py:21
  253.1 2.9 collective-permute-start.3
  253.2 2.8 collective-permute-start.1
  253.6 2.4 collective-permute-start
  254.2 1.8 collective-permute-start.4
Sparse Core Ops, SparseCore 0:
  257.2 74.6 reduce-scatter.1
where the time goes:
time: 342 us; the launch traced here: 341 us
  blocking collectives  263 us (77%)
  waiting for transfers between devices  36.8 us (11%)
  between operations  17.3 us (5%)
  local copies, waits for them, and re-layouts  7.97 us (2%)
  starting transfers between devices  6.36 us (2%)
  other arithmetic  3.98 us (1%)
    all_gather x4, blocking collectives, combined_all(): pieces = jax.tree.map(lambda part: lax.all_gather(part, axis), value)  145 us
    all_gather x1, blocking collectives, local(): lax.all_gather(image, 'grp', axis=0, tiled=True)  43.9 us
    psum x1, blocking collectives, local(): loss = lax.psum(local_loss, ('grp', 'blk')) / (2.0 * total_pairs)  37.2 us
    all_gather x1, blocking collectives, local(): lax.all_gather(mimage, 'grp', axis=0, tiled=True)  37 us
    reduce_scatter x1, waiting for transfers between devices, local(): lax.psum_scatter(image_part, 'grp', scatter_dimension=0, tiled=True)  35 us
  transfers between devices with their start and end apart: 23, of which 5 were waited for; matrix products, arithmetic and copies ran while one was open for 2% of the time, Pallas kernels for 0%

commit v1 on v0

v1 whole, which is shorter than its diff:
```python
import functools

import jax
import jax.numpy as jnp
from jax import lax
from jax.experimental import pallas as pl
from jax.experimental.pallas import tpu as pltpu
from jax.sharding import PartitionSpec as P

mix_weight = 0.4
very_low = -1e30
MESH = pl.DeviceIdType.MESH
f32 = jnp.float32
bf16 = jnp.bfloat16


def lines_of(grp, blk):
    fine = 1
    while fine * blk < grp // fine and grp % (2 * fine) == 0:
        fine *= 2
    return fine


def split_index(index, size):
    if size & (size - 1) == 0:
        return index >> (size.bit_length() - 1), index & (size - 1)
    return lax.div(index, size), lax.rem(index, size)


def kernel(
    grp, blk, fine, rows,
    image_ref, text_ref, mimage_ref, mtext_ref,
    grad_image_ref, grad_text_ref, loss_ref,
    images, texts, image_stats, text_stats, partial, image_out, text_out,
    image_in, text_in, plane_loss_out, line_loss_out, plane_loss, line_loss,
    plane_send, plane_recv, line_send, line_recv,
):
    n_plane, n_line = fine * blk, grp // fine
    width = image_ref.shape[1]
    half = width // 2
    lanes = images.shape[0] * images.shape[1]
    text_rows = n_line * rows
    text_lanes = text_stats.shape[2]
    my_grp, my_blk = lax.axis_index("grp"), lax.axis_index("blk")
    my_line, my_fine = lax.div(my_grp, fine), lax.rem(my_grp, fine)
    my_plane = my_fine * blk + my_blk

    def plane_peer(step):
        rank = lax.rem(my_plane + step, n_plane)
        return rank, (my_line * fine + lax.div(rank, blk), lax.rem(rank, blk))

    def line_peer(step):
        rank = lax.rem(my_line + step, n_line)
        return rank, (rank * fine + my_fine, my_blk)

    plane_peers = [plane_peer(step) for step in range(1, n_plane)]
    line_peers = [line_peer(step) for step in range(1, n_line)]

    def to_plane(phase, step, source, target):
        return pltpu.make_async_remote_copy(
            src_ref=source, dst_ref=target,
            send_sem=plane_send.at[phase, step], recv_sem=plane_recv.at[phase, step],
            device_id=plane_peers[step][1], device_id_type=MESH,
        )

    def to_line(phase, step, source, target):
        return pltpu.make_async_remote_copy(
            src_ref=source, dst_ref=target,
            send_sem=line_send.at[phase, step], recv_sem=line_recv.at[phase, step],
            device_id=line_peers[step][1], device_id_type=MESH,
        )

    def start(copies):
        for copy in copies:
            copy.start()

    def arrived(copies):
        for copy in copies:
            copy.wait_recv()

    barrier = pltpu.get_barrier_semaphore()
    for _, peer in plane_peers + line_peers:
        pl.semaphore_signal(barrier, inc=1, device_id=peer, device_id_type=MESH)

    def pair(first, second):
        return jnp.concatenate([first.astype(f32), second.astype(f32)], axis=0).astype(bf16)

    images[my_plane] = pair(image_ref[...], mimage_ref[...])
    texts[my_line] = pair(text_ref[...], mtext_ref[...])
    pl.semaphore_wait(barrier, n_plane + n_line - 2)

    image_copies = [
        to_plane(0, s, images.at[my_plane], images.at[my_plane]) for s in range(n_plane - 1)
    ]
    text_copies = [to_line(0, s, texts.at[my_line], texts.at[my_line]) for s in range(n_line - 1)]
    start(text_copies)
    start(image_copies)

    shape = (text_rows, lanes)
    text_slot, text_sub = split_index(lax.broadcasted_iota(jnp.int32, shape, 0), rows)
    lane_slot, lane_sub = split_index(lax.broadcasted_iota(jnp.int32, shape, 1), 2 * rows)
    online = lane_sub < rows
    lane_fine, lane_blk = split_index(lane_slot, blk)
    image_tile = lane_blk * grp + my_line * fine + lane_fine
    text_tile = (text_slot * fine + my_fine) * blk + my_blk
    same = (image_tile == text_tile) & (lane_sub == text_sub)
    diagonal = jnp.where(same, 1.0, 0.0)
    square = (text_rows, text_lanes)
    eye = lax.broadcasted_iota(jnp.int32, square, 0) == lax.broadcasted_iota(jnp.int32, square, 1)

    def to_lanes(column):
        return jnp.sum(jnp.where(eye, column, 0.0), axis=0, keepdims=True)

    def to_column(row):
        return jnp.sum(jnp.where(eye, row, 0.0), axis=1, keepdims=True)

    arrived(text_copies)
    arrived(image_copies)
    scores = lax.dot_general(
        texts[...].reshape(n_line * 2 * rows, width), images[...].reshape(lanes, width),
        (((1,), (1,)), ((), ())), preferred_element_type=f32,
    ) * (width ** -0.5)
    scores = scores.reshape(n_line, 2, rows, lanes)
    score_on = scores[:, 0].reshape(shape)
    score_mom = pltpu.roll(scores[:, 1].reshape(shape), lanes - rows, 1)
    masked_on = jnp.where(online, score_on, very_low)
    masked_mom = jnp.where(online, score_mom, very_low)

    def stats(on, mom, axis):
        top_on = jnp.max(on, axis=axis, keepdims=True)
        top_mom = jnp.max(mom, axis=axis, keepdims=True)
        spread = jnp.exp(mom - top_mom)
        return (
            top_on, jnp.sum(jnp.exp(on - top_on), axis=axis, keepdims=True),
            top_mom, jnp.sum(spread, axis=axis, keepdims=True),
            jnp.sum(spread * score_on, axis=axis, keepdims=True),
        )

    def message(top_on, sum_on, top_mom, sum_mom, cross, diag):
        line = lax.broadcasted_iota(jnp.int32, (8, top_on.shape[1]), 0)
        tops = jnp.where(line == 0, top_on, jnp.where((line == 1) | (line == 2), top_mom, 0.0))
        sums = jnp.where(line == 0, sum_on, jnp.where(line == 1, sum_mom, 1.0))
        sums = jnp.where(line == 2, cross, jnp.where(line == 3, diag, sums))
        return jnp.concatenate([tops, sums], axis=0)

    def joined(held, count):
        top = held[0, :8]
        for k in range(1, count):
            top = jnp.maximum(top, held[k, :8])
        total = held[0, 8:] * jnp.exp(held[0, :8] - top)
        for k in range(1, count):
            total = total + held[k, 8:] * jnp.exp(held[k, :8] - top)
        return top + jnp.log(total), total

    text_part = [to_lanes(column) for column in stats(masked_on, masked_mom, 1)]
    in_text = lax.broadcasted_iota(jnp.int32, (1, text_lanes), 1) < text_rows
    for k in (1, 3):
        text_part[k] = jnp.where(in_text, text_part[k], 1.0)
    text_stats[my_line] = message(*text_part, jnp.zeros((1, text_lanes), f32))
    text_copies_1 = [
        to_line(1, s, text_stats.at[my_line], text_stats.at[my_line]) for s in range(n_line - 1)
    ]
    start(text_copies_1)
    diag = jnp.sum(diagonal * score_on, axis=0, keepdims=True)
    image_stats[my_plane] = message(*stats(score_on, score_mom, 0), diag)
    image_copies_1 = [
        to_plane(1, s, image_stats.at[my_plane], image_stats.at[my_plane])
        for s in range(n_plane - 1)
    ]
    start(image_copies_1)
    arrived(text_copies_1)
    text_lse, text_total = joined(text_stats, n_line)
    col_on, col_mom = to_column(text_lse[0:1]), to_column(text_lse[1:2])
    prob_col = jnp.exp(masked_on - col_on)
    target_col = mix_weight * jnp.exp(masked_mom - col_mom) + (1.0 - mix_weight) * diagonal
    arrived(image_copies_1)
    image_lse, image_total = joined(image_stats, n_plane)
    prob_row = jnp.exp(score_on - image_lse[0:1])
    target_row = (
        mix_weight * jnp.exp(score_mom - image_lse[1:2]) + (1.0 - mix_weight) * diagonal
    )
    grad = 0.5 * ((prob_row - target_row) + (prob_col - target_col))
    grad = jnp.where(online, grad, 0.0)

    spaced = jnp.concatenate(
        [grad.reshape(n_line, 1, rows, lanes), jnp.zeros((n_line, 1, rows, lanes), f32)], axis=1
    ).reshape(n_line * 2 * rows, lanes)
    partial[...] = lax.dot_general(
        spaced.astype(bf16), texts[...].reshape(n_line * 2 * rows, width),
        (((0,), (0,)), ((), ())), preferred_element_type=f32,
    ).reshape(n_plane, 2 * rows, width)

    def folded(value):
        return jnp.concatenate([value[:, :half], value[:, half:]], axis=0).astype(bf16)

    image_copies_2 = []
    for s in range(n_plane - 1):
        image_out[s] = folded(partial[plane_peers[s][0], :rows, :])
        copy = to_plane(2, s, image_out.at[s], image_in.at[s])
        copy.start()
        image_copies_2.append(copy)

    text_share = jnp.dot(
        grad.astype(bf16), images[...].reshape(lanes, width), preferred_element_type=f32
    )
    own_image = partial[my_plane, :rows, :]
    partial[pl.ds(0, n_line), :rows, :] = text_share.reshape(n_line, rows, width)
    text_copies_2 = []
    for s in range(n_line - 1):
        text_out[s] = folded(partial[line_peers[s][0], :rows, :])
        copy = to_line(2, s, text_out.at[s], text_in.at[s])
        copy.start()
        text_copies_2.append(copy)
    own_text = partial[my_line, :rows, :]

    def shares(lse, total, valid):
        share = lse[0:1] - mix_weight * (total[2:3] / total[1:2])
        return jnp.where(valid, share, 0.0)

    image_share = shares(image_lse, image_total, online[0:1])
    image_share = image_share - jnp.where(
        online[0:1], 2.0 * (1.0 - mix_weight) * image_total[3:4], 0.0
    )
    text_loss = shares(text_lse, text_total, in_text)
    line = lax.broadcasted_iota(jnp.int32, (8, lanes), 0)
    line_loss_out[...] = jnp.where(line == 0, image_share, 0.0)
    line = lax.broadcasted_iota(jnp.int32, (8, text_lanes), 0)
    plane_loss_out[...] = jnp.where(line == 0, text_loss, 0.0)
    line_copies_3 = [
        to_line(3, s, line_loss_out, line_loss.at[s]) for s in range(n_line - 1)
    ]
    plane_copies_3 = [
        to_plane(3, s, plane_loss_out, plane_loss.at[s]) for s in range(n_plane - 1)
    ]
    start(line_copies_3)
    start(plane_copies_3)

    def gathered(own, held, count):
        total = jnp.concatenate([own[:, :half], own[:, half:]], axis=0)
        for s in range(count):
            total = total + held[s].astype(f32)
        return jnp.concatenate([total[:rows], total[rows:]], axis=1)

    arrived(image_copies_2)
    grad_image_ref[...] = gathered(own_image, image_in, n_plane - 1)
    arrived(text_copies_2)
    grad_text_ref[...] = gathered(own_text, text_in, n_line - 1)
    arrived(line_copies_3)
    arrived(plane_copies_3)
    image_loss = line_loss_out[...]
    for s in range(n_line - 1):
        image_loss = image_loss + line_loss[s]
    text_loss = plane_loss_out[...]
    for s in range(n_plane - 1):
        text_loss = text_loss + plane_loss[s]
    total = jnp.sum(image_loss, keepdims=True) + jnp.sum(text_loss, keepdims=True)
    loss_ref[...] = total / (2.0 * rows * grp * blk)

    for copy in (
        image_copies + text_copies + image_copies_1 + text_copies_1
        + image_copies_2 + text_copies_2 + line_copies_3 + plane_copies_3
    ):
        copy.wait_send()


def local(grp, blk, image, text, mimage, mtext):
    rows, width = image.shape
    fine = lines_of(grp, blk)
    n_plane, n_line = fine * blk, grp // fine
    lanes = n_plane * 2 * rows
    text_lanes = -(-n_line * rows // 128) * 128
    in_vmem = pl.BlockSpec(memory_space=pltpu.VMEM)
    grad_image, grad_text, loss = pl.pallas_call(
        functools.partial(kernel, grp, blk, fine, rows),
        out_shape=(
            jax.ShapeDtypeStruct((rows, width), f32),
            jax.ShapeDtypeStruct((rows, width), f32),
            jax.ShapeDtypeStruct((1, 1), f32),
        ),
        in_specs=[in_vmem] * 4,
        out_specs=(in_vmem, in_vmem, in_vmem),
        scratch_shapes=[
            pltpu.VMEM((n_plane, 2 * rows, width), bf16),
            pltpu.VMEM((n_line, 2 * rows, width), bf16),
            pltpu.VMEM((n_plane, 16, lanes), f32),
            pltpu.VMEM((n_line, 16, text_lanes), f32),
            pltpu.VMEM((max(n_plane, n_line), 2 * rows, width), f32),
            pltpu.VMEM((n_plane - 1, 2 * rows, width // 2), bf16),
            pltpu.VMEM((n_line - 1, 2 * rows, width // 2), bf16),
            pltpu.VMEM((n_plane - 1, 2 * rows, width // 2), bf16),
            pltpu.VMEM((n_line - 1, 2 * rows, width // 2), bf16),
            pltpu.VMEM((8, text_lanes), f32),
            pltpu.VMEM((8, lanes), f32),
            pltpu.VMEM((n_plane - 1, 8, text_lanes), f32),
            pltpu.VMEM((n_line - 1, 8, lanes), f32),
            pltpu.SemaphoreType.DMA((4, n_plane - 1)),
            pltpu.SemaphoreType.DMA((4, n_plane - 1)),
            pltpu.SemaphoreType.DMA((4, n_line - 1)),
            pltpu.SemaphoreType.DMA((4, n_line - 1)),
        ],
        compiler_params=pltpu.CompilerParams(
            collective_id=0, has_side_effects=True, vmem_limit_bytes=32 * 1024 * 1024
        ),
    )(image, text, mimage, mtext)
    return grad_image, grad_text, loss.reshape(())


def solution(mesh):
    in_specs = (
        P(("blk", "grp"), None),
        P(("grp", "blk"), None),
        P(("blk", "grp"), None),
        P(("grp", "blk"), None),
    )
    out_specs = (P(("blk", "grp"), None), P(("grp", "blk"), None), P())
    run = functools.partial(local, mesh.shape["grp"], mesh.shape["blk"])
    return jax.shard_map(run, mesh=mesh, in_specs=in_specs, out_specs=out_specs, check_vma=False)
```

time: 342 us -> 27.4 us (0.08)
  blocking collectives: 263 us -> 0 us
  waiting for transfers between devices: 36.8 us -> 0 us
  Pallas kernels: 0 us -> 20.4 us
  between operations: 17.3 us -> 2.4 us
  starting transfers between devices: 6.36 us -> 0 us
  other arithmetic: 3.98 us -> 0 us
  local copies, waits for them, and re-layouts: 7.97 us -> 4.09 us
    all_gather x6 -> x0, blocking collectives: 226 us -> none  [the longest x4 145 us: combined_all(): pieces = jax.tree.map(lambda part: lax.all_gather(part, axis), value)]
    psum x1 -> x0, blocking collectives: 37.2 us -> none  [local(): loss = lax.psum(local_loss, ('grp', 'blk')) / (2.0 * total_pairs)]
    reduce_scatter x1 -> x0, waiting for transfers between devices: 35 us -> none  [local(): lax.psum_scatter(image_part, 'grp', scatter_dimension=0, tiled=True)]
    pallas_call x0 -> x1, Pallas kernels: none -> 20.4 us  [local(): pl.pallas_call(functools.partial(kernel, grp, blk, fine, rows), out_shape...]
    ppermute x22 -> x0, starting transfers between devices: 6.33 us -> none  [from_behind(): return lax.ppermute(value, axis, pairs)]
  transfers between devices with their start and end apart: 23 -> 0, of which waited for: 5 -> 0; matrix products, arithmetic and copies ran while one was open for 2% -> 0% of each run, Pallas kernels for 0% -> 0%
where the time goes in v1:
time: 27.4 us; the launch traced here: 26.9 us
  Pallas kernels  20.4 us (74%)
  local copies, waits for them, and re-layouts  4.09 us (15%)
  between operations  2.4 us (9%)
    pallas_call x1, Pallas kernels, local(): pl.pallas_call(functools.partial(kernel, grp, blk, fine, rows), out_shape...  20.4 us
    unnamed x10, local copies, waits for them, and re-layouts  4.09 us

profile of v1, /device:TPU:0, one launch (start us, length us, event | category | flops | bytes accessed | tf_op | source)
XLA Modules:
  0.0 26.9 jit_solution(299426060676603957)
XLA Ops:
  0.6 0.0 copy-start
  0.6 0.7 %copy-done = bf16[8,1024]{1,0:T(8,128)(2,1)S(1)} copy-done((bf16[8,1024]{1,0:T(8,128)(2,1)S(1)}, bf16[8,1024]{1,0:T(8,128)(2,1)}, u32[]{:S(2)}) %copy-start) | copy-done | bytes 16408
  1.3 0.0 copy-start.1
  1.4 0.7 %copy-done.1 = bf16[8,1024]{1,0:T(8,128)(2,1)S(1)} copy-done((bf16[8,1024]{1,0:T(8,128)(2,1)S(1)}, bf16[8,1024]{1,0:T(8,128)(2,1)}, u32[]{:S(2)}) %copy-start.1) | copy-done | bytes 16408
  2.1 0.0 copy-start.2
  2.1 0.7 %copy-done.2 = bf16[8,1024]{1,0:T(8,128)(2,1)S(1)} copy-done((bf16[8,1024]{1,0:T(8,128)(2,1)S(1)}, bf16[8,1024]{1,0:T(8,128)(2,1)}, u32[]{:S(2)}) %copy-start.2) | copy-done | bytes 16408
  2.8 0.0 copy-start.3
  2.8 0.7 %copy-done.3 = bf16[8,1024]{1,0:T(8,128)(2,1)S(1)} copy-done((bf16[8,1024]{1,0:T(8,128)(2,1)S(1)}, bf16[8,1024]{1,0:T(8,128)(2,1)}, u32[]{:S(2)}) %copy-start.3) | copy-done | bytes 16408
  3.5 20.4 %shard_map.67 = (f32[8,1024]{1,0:T(8,128)S(1)}, f32[8,1024]{1,0:T(8,128)S(1)}, f32[1,1]{1,0:T(1,128)}) custom-call(bf16[8,1024]{1,0:T(8,128)(2,1)S(1)} %copy-done, bf16[8,1024]{1,0:T(8,128)(2,1)S(1)} %copy-done.1, bf16[8,1024]{1,0:T(8,128)(2,1)S(1)} %copy-done.2, bf16[8,1024]{1,0:T(8,128)(2,1)S(1)} %copy-done.3), custom_call_target="tpu_custom_call" | custom-call | tf_op jit(solution)/shard_map/pallas_call | solution.py:273
  23.9 0.6 %copy.10 = f32[8,1024]{1,0:T(8,128)} copy(f32[8,1024]{1,0:T(8,128)S(1)} %get-tuple-element.12) | data formatting | bytes 65536
  24.5 0.6 %copy.11 = f32[8,1024]{1,0:T(8,128)} copy(f32[8,1024]{1,0:T(8,128)S(1)} %get-tuple-element.13) | data formatting | bytes 65536
Async XLA Ops:
  0.6 0.7 %copy-start = (bf16[8,1024]{1,0:T(8,128)(2,1)S(1)}, bf16[8,1024]{1,0:T(8,128)(2,1)}, u32[]{:S(2)}) copy-start(bf16[8,1024]{1,0:T(8,128)(2,1)} %image_ref.1) | copy-start | bytes 49156
  1.3 0.7 %copy-start.1 = (bf16[8,1024]{1,0:T(8,128)(2,1)S(1)}, bf16[8,1024]{1,0:T(8,128)(2,1)}, u32[]{:S(2)}) copy-start(bf16[8,1024]{1,0:T(8,128)(2,1)} %text_ref.1) | copy-start | bytes 49156
  2.1 0.7 %copy-start.2 = (bf16[8,1024]{1,0:T(8,128)(2,1)S(1)}, bf16[8,1024]{1,0:T(8,128)(2,1)}, u32[]{:S(2)}) copy-start(bf16[8,1024]{1,0:T(8,128)(2,1)} %mimage_ref.1) | copy-start | bytes 49156
  2.8 0.7 %copy-start.3 = (bf16[8,1024]{1,0:T(8,128)(2,1)S(1)}, bf16[8,1024]{1,0:T(8,128)(2,1)}, u32[]{:S(2)}) copy-start(bf16[8,1024]{1,0:T(8,128)(2,1)} %mtext_ref.1) | copy-start | bytes 49156

commit v2 on v1

--- a/solution.py
+++ b/solution.py
@@ -31,10 +31,16 @@
     grp, blk, fine, rows,
     image_ref, text_ref, mimage_ref, mtext_ref,
     grad_image_ref, grad_text_ref, loss_ref,
-    images, texts, image_stats, text_stats, partial, image_out, text_out,
+    images, texts, image_stats, text_stats, plane_partial, line_partial, image_out, text_out,
     image_in, text_in, plane_loss_out, line_loss_out, plane_loss, line_loss,
-    plane_send, plane_recv, line_send, line_recv,
+    plane_send, plane_recv, line_send, line_recv, fetched, fetch_sem,
 ):
+    fetches = [
+        pltpu.make_async_copy(ref, fetched.at[k], fetch_sem.at[k])
+        for k, ref in enumerate((text_ref, mtext_ref, image_ref, mimage_ref))
+    ]
+    for copy in fetches:
+        copy.start()
     n_plane, n_line = fine * blk, grp // fine
     width = image_ref.shape[1]
     half = width // 2
@@ -85,8 +91,10 @@
     def pair(first, second):
         return jnp.concatenate([first.astype(f32), second.astype(f32)], axis=0).astype(bf16)
 
-    images[my_plane] = pair(image_ref[...], mimage_ref[...])
-    texts[my_line] = pair(text_ref[...], mtext_ref[...])
+    for copy in fetches:
+        copy.wait()
+    texts[my_line] = pair(fetched[0], fetched[1])
+    images[my_plane] = pair(fetched[2], fetched[3])
     pl.semaphore_wait(barrier, n_plane + n_line - 2)
 
     image_copies = [
@@ -182,36 +190,31 @@
     grad = 0.5 * ((prob_row - target_row) + (prob_col - target_col))
     grad = jnp.where(online, grad, 0.0)
 
+    def folded(value):
+        return jnp.concatenate([value[:, :half], value[:, half:]], axis=0).astype(bf16)
+
+    line_partial[...] = jnp.dot(
+        grad.astype(bf16), images[...].reshape(lanes, width), preferred_element_type=f32
+    ).reshape(n_line, rows, width)
+    text_copies_2 = []
+    for s in range(n_line - 1):
+        text_out[s] = folded(line_partial[line_peers[s][0]])
+        copy = to_line(2, s, text_out.at[s], text_in.at[s])
+        copy.start()
+        text_copies_2.append(copy)
     spaced = jnp.concatenate(
         [grad.reshape(n_line, 1, rows, lanes), jnp.zeros((n_line, 1, rows, lanes), f32)], axis=1
     ).reshape(n_line * 2 * rows, lanes)
-    partial[...] = lax.dot_general(
+    plane_partial[...] = lax.dot_general(
         spaced.astype(bf16), texts[...].reshape(n_line * 2 * rows, width),
         (((0,), (0,)), ((), ())), preferred_element_type=f32,
     ).reshape(n_plane, 2 * rows, width)
-
-    def folded(value):
-        return jnp.concatenate([value[:, :half], value[:, half:]], axis=0).astype(bf16)
-
     image_copies_2 = []
     for s in range(n_plane - 1):
-        image_out[s] = folded(partial[plane_peers[s][0], :rows, :])
+        image_out[s] = folded(plane_partial[plane_peers[s][0], :rows, :])
         copy = to_plane(2, s, image_out.at[s], image_in.at[s])
         copy.start()
         image_copies_2.append(copy)
-
-    text_share = jnp.dot(
-        grad.astype(bf16), images[...].reshape(lanes, width), preferred_element_type=f32
-    )
-    own_image = partial[my_plane, :rows, :]
-    partial[pl.ds(0, n_line), :rows, :] = text_share.reshape(n_line, rows, width)
-    text_copies_2 = []
-    for s in range(n_line - 1):
-        text_out[s] = folded(partial[line_peers[s][0], :rows, :])
-        copy = to_line(2, s, text_out.at[s], text_in.at[s])
-        copy.start()
-        text_copies_2.append(copy)
-    own_text = partial[my_line, :rows, :]
 
     def shares(lse, total, valid):
         share = lse[0:1] - mix_weight * (total[2:3] / total[1:2])
@@ -241,10 +244,10 @@
             total = total + held[s].astype(f32)
         return jnp.concatenate([total[:rows], total[rows:]], axis=1)
 
+    arrived(text_copies_2)
+    grad_text_ref[...] = gathered(line_partial[my_line], text_in, n_line - 1)
     arrived(image_copies_2)
-    grad_image_ref[...] = gathered(own_image, image_in, n_plane - 1)
-    arrived(text_copies_2)
-    grad_text_ref[...] = gathered(own_text, text_in, n_line - 1)
+    grad_image_ref[...] = gathered(plane_partial[my_plane, :rows, :], image_in, n_plane - 1)
     arrived(line_copies_3)
     arrived(plane_copies_3)
     image_loss = line_loss_out[...]
@@ -277,14 +280,15 @@
             jax.ShapeDtypeStruct((rows, width), f32),
             jax.ShapeDtypeStruct((1, 1), f32),
         ),
-        in_specs=[in_vmem] * 4,
+        in_specs=[pl.BlockSpec(memory_space=pltpu.HBM)] * 4,
         out_specs=(in_vmem, in_vmem, in_vmem),
         scratch_shapes=[
             pltpu.VMEM((n_plane, 2 * rows, width), bf16),
             pltpu.VMEM((n_line, 2 * rows, width), bf16),
             pltpu.VMEM((n_plane, 16, lanes), f32),
             pltpu.VMEM((n_line, 16, text_lanes), f32),
-            pltpu.VMEM((max(n_plane, n_line), 2 * rows, width), f32),
+            pltpu.VMEM((n_plane, 2 * rows, width), f32),
+            pltpu.VMEM((n_line, rows, width), f32),
             pltpu.VMEM((n_plane - 1, 2 * rows, width // 2), bf16),
             pltpu.VMEM((n_line - 1, 2 * rows, width // 2), bf16),
             pltpu.VMEM((n_plane - 1, 2 * rows, width // 2), bf16),
@@ -297,6 +301,8 @@
             pltpu.SemaphoreType.DMA((4, n_plane - 1)),
             pltpu.SemaphoreType.DMA((4, n_line - 1)),
             pltpu.SemaphoreType.DMA((4, n_line - 1)),
+            pltpu.VMEM((4, rows, width), bf16),
+            pltpu.SemaphoreType.DMA((4,)),
         ],
         compiler_params=pltpu.CompilerParams(
             collective_id=0, has_side_effects=True, vmem_limit_bytes=32 * 1024 * 1024

time: 27.4 us -> 27.7 us (1.011)
  Pallas kernels: 20.4 us -> 20.7 us
    pallas_call x1, Pallas kernels: 20.4 us -> 20.7 us  [local(): pl.pallas_call(functools.partial(kernel, grp, blk, fine, rows), out_shape...]
where the time goes in v2:
time: 27.7 us; the launch traced here: 27.2 us
  Pallas kernels  20.7 us (75%)
  local copies, waits for them, and re-layouts  4.09 us (15%)
  between operations  2.4 us (9%)
    pallas_call x1, Pallas kernels, local(): pl.pallas_call(functools.partial(kernel, grp, blk, fine, rows), out_shape...  20.7 us
    unnamed x10, local copies, waits for them, and re-layouts  4.09 us

profile of v2, /device:TPU:0, one launch (start us, length us, event | category | flops | bytes accessed | tf_op | source)
XLA Modules:
  0.0 27.2 jit_solution(1487940414266055697)
XLA Ops:
  0.6 0.0 copy-start
  0.6 0.7 %copy-done = bf16[8,1024]{1,0:T(8,128)(2,1)S(1)} copy-done((bf16[8,1024]{1,0:T(8,128)(2,1)S(1)}, bf16[8,1024]{1,0:T(8,128)(2,1)}, u32[]{:S(2)}) %copy-start) | copy-done | bytes 16408
  1.3 0.0 copy-start.1
  1.4 0.7 %copy-done.1 = bf16[8,1024]{1,0:T(8,128)(2,1)S(1)} copy-done((bf16[8,1024]{1,0:T(8,128)(2,1)S(1)}, bf16[8,1024]{1,0:T(8,128)(2,1)}, u32[]{:S(2)}) %copy-start.1) | copy-done | bytes 16408
  2.1 0.0 copy-start.2
  2.1 0.7 %copy-done.2 = bf16[8,1024]{1,0:T(8,128)(2,1)S(1)} copy-done((bf16[8,1024]{1,0:T(8,128)(2,1)S(1)}, bf16[8,1024]{1,0:T(8,128)(2,1)}, u32[]{:S(2)}) %copy-start.2) | copy-done | bytes 16408
  2.8 0.0 copy-start.3
  2.8 0.7 %copy-done.3 = bf16[8,1024]{1,0:T(8,128)(2,1)S(1)} copy-done((bf16[8,1024]{1,0:T(8,128)(2,1)S(1)}, bf16[8,1024]{1,0:T(8,128)(2,1)}, u32[]{:S(2)}) %copy-start.3) | copy-done | bytes 16408
  3.5 20.7 %shard_map.67 = (f32[8,1024]{1,0:T(8,128)S(1)}, f32[8,1024]{1,0:T(8,128)S(1)}, f32[1,1]{1,0:T(1,128)}) custom-call(bf16[8,1024]{1,0:T(8,128)(2,1)S(1)} %copy-done, bf16[8,1024]{1,0:T(8,128)(2,1)S(1)} %copy-done.1, bf16[8,1024]{1,0:T(8,128)(2,1)S(1)} %copy-done.2, bf16[8,1024]{1,0:T(8,128)(2,1)S(1)} %copy-done.3), custom_call_target="tpu_custom_call" | custom-call | tf_op jit(solution)/shard_map/pallas_call | solution.py:276
  24.2 0.6 %copy.10 = f32[8,1024]{1,0:T(8,128)} copy(f32[8,1024]{1,0:T(8,128)S(1)} %get-tuple-element.12) | data formatting | bytes 65536
  24.8 0.6 %copy.11 = f32[8,1024]{1,0:T(8,128)} copy(f32[8,1024]{1,0:T(8,128)S(1)} %get-tuple-element.13) | data formatting | bytes 65536
Async XLA Ops:
  0.6 0.7 %copy-start = (bf16[8,1024]{1,0:T(8,128)(2,1)S(1)}, bf16[8,1024]{1,0:T(8,128)(2,1)}, u32[]{:S(2)}) copy-start(bf16[8,1024]{1,0:T(8,128)(2,1)} %image_ref.1) | copy-start | bytes 49156
  1.3 0.7 %copy-start.1 = (bf16[8,1024]{1,0:T(8,128)(2,1)S(1)}, bf16[8,1024]{1,0:T(8,128)(2,1)}, u32[]{:S(2)}) copy-start(bf16[8,1024]{1,0:T(8,128)(2,1)} %text_ref.1) | copy-start | bytes 49156
  2.1 0.7 %copy-start.2 = (bf16[8,1024]{1,0:T(8,128)(2,1)S(1)}, bf16[8,1024]{1,0:T(8,128)(2,1)}, u32[]{:S(2)}) copy-start(bf16[8,1024]{1,0:T(8,128)(2,1)} %mimage_ref.1) | copy-start | bytes 49156
  2.8 0.7 %copy-start.3 = (bf16[8,1024]{1,0:T(8,128)(2,1)S(1)}, bf16[8,1024]{1,0:T(8,128)(2,1)}, u32[]{:S(2)}) copy-start(bf16[8,1024]{1,0:T(8,128)(2,1)} %mtext_ref.1) | copy-start | bytes 49156

commit v3 on v2

--- a/solution.py
+++ b/solution.py
@@ -33,7 +33,7 @@
     grad_image_ref, grad_text_ref, loss_ref,
     images, texts, image_stats, text_stats, plane_partial, line_partial, image_out, text_out,
     image_in, text_in, plane_loss_out, line_loss_out, plane_loss, line_loss,
-    plane_send, plane_recv, line_send, line_recv, fetched, fetch_sem,
+    plane_send, plane_recv, line_send, line_recv, fetched, fetch_sem, result, result_sem,
 ):
     fetches = [
         pltpu.make_async_copy(ref, fetched.at[k], fetch_sem.at[k])
@@ -245,9 +245,15 @@
         return jnp.concatenate([total[:rows], total[rows:]], axis=1)
 
     arrived(text_copies_2)
-    grad_text_ref[...] = gathered(line_partial[my_line], text_in, n_line - 1)
+    result[0] = gathered(line_partial[my_line], text_in, n_line - 1)
+    results = [
+        pltpu.make_async_copy(result.at[0], grad_text_ref, result_sem.at[0]),
+        pltpu.make_async_copy(result.at[1], grad_image_ref, result_sem.at[1]),
+    ]
+    results[0].start()
     arrived(image_copies_2)
-    grad_image_ref[...] = gathered(plane_partial[my_plane, :rows, :], image_in, n_plane - 1)
+    result[1] = gathered(plane_partial[my_plane, :rows, :], image_in, n_plane - 1)
+    results[1].start()
     arrived(line_copies_3)
     arrived(plane_copies_3)
     image_loss = line_loss_out[...]
@@ -264,6 +270,8 @@
         + image_copies_2 + text_copies_2 + line_copies_3 + plane_copies_3
     ):
         copy.wait_send()
+    for copy in results:
+        copy.wait()
 
 
 def local(grp, blk, image, text, mimage, mtext):
@@ -272,6 +280,7 @@
     n_plane, n_line = fine * blk, grp // fine
     lanes = n_plane * 2 * rows
     text_lanes = -(-n_line * rows // 128) * 128
+    in_hbm = pl.BlockSpec(memory_space=pltpu.HBM)
     in_vmem = pl.BlockSpec(memory_space=pltpu.VMEM)
     grad_image, grad_text, loss = pl.pallas_call(
         functools.partial(kernel, grp, blk, fine, rows),
@@ -280,8 +289,8 @@
             jax.ShapeDtypeStruct((rows, width), f32),
             jax.ShapeDtypeStruct((1, 1), f32),
         ),
-        in_specs=[pl.BlockSpec(memory_space=pltpu.HBM)] * 4,
-        out_specs=(in_vmem, in_vmem, in_vmem),
+        in_specs=[in_hbm] * 4,
+        out_specs=(in_hbm, in_hbm, in_vmem),
         scratch_shapes=[
             pltpu.VMEM((n_plane, 2 * rows, width), bf16),
             pltpu.VMEM((n_line, 2 * rows, width), bf16),
@@ -303,9 +312,11 @@
             pltpu.SemaphoreType.DMA((4, n_line - 1)),
             pltpu.VMEM((4, rows, width), bf16),
             pltpu.SemaphoreType.DMA((4,)),
+            pltpu.VMEM((2, rows, width), f32),
+            pltpu.SemaphoreType.DMA((2,)),
         ],
         compiler_params=pltpu.CompilerParams(
-            collective_id=0, has_side_effects=True, vmem_limit_bytes=32 * 1024 * 1024
+            collective_id=0, has_side_effects=True, vmem_limit_bytes=60 * 1024 * 1024
         ),
     )(image, text, mimage, mtext)
     return grad_image, grad_text, loss.reshape(())

time: 27.7 us -> 25.4 us (0.917)
  local copies, waits for them, and re-layouts: 4.09 us -> 2 us
    unnamed x10 -> x4, local copies, waits for them, and re-layouts: 4.09 us -> 2 us
where the time goes in v3:
time: 25.4 us; the launch traced here: 25 us
  Pallas kernels  20.7 us (81%)
  between operations  2.34 us (9%)
  local copies, waits for them, and re-layouts  2 us (8%)
    pallas_call x1, Pallas kernels, local(): pl.pallas_call(functools.partial(kernel, grp, blk, fine, rows), out_shape...  20.7 us
    unnamed x4, local copies, waits for them, and re-layouts  2 us

profile of v3, /device:TPU:0, one launch (start us, length us, event | category | flops | bytes accessed | tf_op | source)
XLA Modules:
  0.0 25.0 jit_solution(17789984107324958427)
XLA Ops:
  0.6 20.7 %shard_map.67 = (f32[8,1024]{1,0:T(8,128)}, f32[8,1024]{1,0:T(8,128)}, f32[1,1]{1,0:T(1,128)}) custom-call(bf16[8,1024]{1,0:T(8,128)(2,1)} %image_ref.1, bf16[8,1024]{1,0:T(8,128)(2,1)} %text_ref.1, bf16[8,1024]{1,0:T(8,128)(2,1)} %mimage_ref.1, bf16[8,1024]{1,0:T(8,128)(2,1)} %mtext_ref.1), custom_call_target="tpu_custom_call" | custom-call | tf_op jit(solution)/shard_map/pallas_call | solution.py:285
  21.3 0.0 copy-start
  21.3 1.4 %copy.10 = f32[8,1024]{1,0:T(8,128)} copy(f32[8,1024]{1,0:T(8,128)} %get-tuple-element.12) | data formatting | bytes 65536
  22.7 0.0 copy-done
  22.7 0.6 %copy.11 = f32[8,1024]{1,0:T(8,128)} copy(f32[8,1024]{1,0:T(8,128)S(1)} %copy-done) | data formatting | bytes 65536
Async XLA Ops:
  21.3 1.4 %copy-start = (f32[8,1024]{1,0:T(8,128)S(1)}, f32[8,1024]{1,0:T(8,128)}, u32[]{:S(2)}) copy-start(f32[8,1024]{1,0:T(8,128)} %get-tuple-element.13) | copy-start | bytes 98308

commit v4 on v3

--- a/solution.py
+++ b/solution.py
@@ -35,12 +35,6 @@
     image_in, text_in, plane_loss_out, line_loss_out, plane_loss, line_loss,
     plane_send, plane_recv, line_send, line_recv, fetched, fetch_sem, result, result_sem,
 ):
-    fetches = [
-        pltpu.make_async_copy(ref, fetched.at[k], fetch_sem.at[k])
-        for k, ref in enumerate((text_ref, mtext_ref, image_ref, mimage_ref))
-    ]
-    for copy in fetches:
-        copy.start()
     n_plane, n_line = fine * blk, grp // fine
     width = image_ref.shape[1]
     half = width // 2
@@ -59,34 +53,57 @@
         rank = lax.rem(my_line + step, n_line)
         return rank, (rank * fine + my_fine, my_blk)
 
-    plane_peers = [plane_peer(step) for step in range(1, n_plane)]
-    line_peers = [line_peer(step) for step in range(1, n_line)]
-
-    def to_plane(phase, step, source, target):
-        return pltpu.make_async_remote_copy(
-            src_ref=source, dst_ref=target,
-            send_sem=plane_send.at[phase, step], recv_sem=plane_recv.at[phase, step],
-            device_id=plane_peers[step][1], device_id_type=MESH,
-        )
-
-    def to_line(phase, step, source, target):
-        return pltpu.make_async_remote_copy(
-            src_ref=source, dst_ref=target,
-            send_sem=line_send.at[phase, step], recv_sem=line_recv.at[phase, step],
-            device_id=line_peers[step][1], device_id_type=MESH,
-        )
-
-    def start(copies):
-        for copy in copies:
-            copy.start()
-
-    def arrived(copies):
-        for copy in copies:
-            copy.wait_recv()
+    def send_all(peer_of, count, sems, phase, ends):
+        send_sem, recv_sem = sems
+
+        def step(s, carry):
+            rank, peer = peer_of(s + 1)
+            source, target = ends(s, rank)
+            pltpu.make_async_remote_copy(
+                src_ref=source, dst_ref=target,
+                send_sem=send_sem.at[phase], recv_sem=recv_sem.at[phase],
+                device_id=peer, device_id_type=MESH,
+            ).start()
+            return carry
+
+        lax.fori_loop(0, count - 1, step, 0)
+
+    def wait_all(sem, phase, span):
+        pltpu.make_async_copy(span, span, sem.at[phase]).wait()
+
+    plane_sems, line_sems = (plane_send, plane_recv), (line_send, line_recv)
+
+    def to_plane(phase, ends):
+        send_all(plane_peer, n_plane, plane_sems, phase, ends)
+
+    def to_line(phase, ends):
+        send_all(line_peer, n_line, line_sems, phase, ends)
+
+    other_planes, other_lines = pl.ds(0, n_plane - 1), pl.ds(0, n_line - 1)
+    plane_spans = [
+        images.at[other_planes], image_stats.at[other_planes], image_in, plane_loss,
+    ]
+    line_spans = [texts.at[other_lines], text_stats.at[other_lines], text_in, line_loss]
 
     barrier = pltpu.get_barrier_semaphore()
-    for _, peer in plane_peers + line_peers:
-        pl.semaphore_signal(barrier, inc=1, device_id=peer, device_id_type=MESH)
+
+    def greet(peer_of, count):
+        def step(s, carry):
+            pl.semaphore_signal(
+                barrier, inc=1, device_id=peer_of(s + 1)[1], device_id_type=MESH
+            )
+            return carry
+
+        lax.fori_loop(0, count - 1, step, 0)
+
+    greet(line_peer, n_line)
+    greet(plane_peer, n_plane)
+    fetches = [
+        pltpu.make_async_copy(ref, fetched.at[k], fetch_sem.at[k])
+        for k, ref in enumerate((text_ref, mtext_ref, image_ref, mimage_ref))
+    ]
+    for copy in fetches:
+        copy.start()
 
     def pair(first, second):
         return jnp.concatenate([first.astype(f32), second.astype(f32)], axis=0).astype(bf16)
@@ -97,12 +114,8 @@
     images[my_plane] = pair(fetched[2], fetched[3])
     pl.semaphore_wait(barrier, n_plane + n_line - 2)
 
-    image_copies = [
-        to_plane(0, s, images.at[my_plane], images.at[my_plane]) for s in range(n_plane - 1)
-    ]
-    text_copies = [to_line(0, s, texts.at[my_line], texts.at[my_line]) for s in range(n_line - 1)]
-    start(text_copies)
-    start(image_copies)
+    to_line(0, lambda s, rank: (texts.at[my_line], texts.at[my_line]))
+    to_plane(0, lambda s, rank: (images.at[my_plane], images.at[my_plane]))
 
     shape = (text_rows, lanes)
     text_slot, text_sub = split_index(lax.broadcasted_iota(jnp.int32, shape, 0), rows)
@@ -122,8 +135,8 @@
     def to_column(row):
         return jnp.sum(jnp.where(eye, row, 0.0), axis=1, keepdims=True)
 
-    arrived(text_copies)
-    arrived(image_copies)
+    wait_all(line_recv, 0, line_spans[0])
+    wait_all(plane_recv, 0, plane_spans[0])
     scores = lax.dot_general(
         texts[...].reshape(n_line * 2 * rows, width), images[...].reshape(lanes, width),
         (((1,), (1,)), ((), ())), preferred_element_type=f32,
@@ -165,23 +178,16 @@
     for k in (1, 3):
         text_part[k] = jnp.where(in_text, text_part[k], 1.0)
     text_stats[my_line] = message(*text_part, jnp.zeros((1, text_lanes), f32))
-    text_copies_1 = [
-        to_line(1, s, text_stats.at[my_line], text_stats.at[my_line]) for s in range(n_line - 1)
-    ]
-    start(text_copies_1)
+    to_line(1, lambda s, rank: (text_stats.at[my_line], text_stats.at[my_line]))
     diag = jnp.sum(diagonal * score_on, axis=0, keepdims=True)
     image_stats[my_plane] = message(*stats(score_on, score_mom, 0), diag)
-    image_copies_1 = [
-        to_plane(1, s, image_stats.at[my_plane], image_stats.at[my_plane])
-        for s in range(n_plane - 1)
-    ]
-    start(image_copies_1)
-    arrived(text_copies_1)
+    to_plane(1, lambda s, rank: (image_stats.at[my_plane], image_stats.at[my_plane]))
+    wait_all(line_recv, 1, line_spans[1])
     text_lse, text_total = joined(text_stats, n_line)
     col_on, col_mom = to_column(text_lse[0:1]), to_column(text_lse[1:2])
     prob_col = jnp.exp(masked_on - col_on)
     target_col = mix_weight * jnp.exp(masked_mom - col_mom) + (1.0 - mix_weight) * diagonal
-    arrived(image_copies_1)
+    wait_all(plane_recv, 1, plane_spans[1])
     image_lse, image_total = joined(image_stats, n_plane)
     prob_row = jnp.exp(score_on - image_lse[0:1])
     target_row = (
@@ -196,12 +202,12 @@
     line_partial[...] = jnp.dot(
         grad.astype(bf16), images[...].reshape(lanes, width), preferred_element_type=f32
     ).reshape(n_line, rows, width)
-    text_copies_2 = []
-    for s in range(n_line - 1):
-        text_out[s] = folded(line_partial[line_peers[s][0]])
-        copy = to_line(2, s, text_out.at[s], text_in.at[s])
-        copy.start()
-        text_copies_2.append(copy)
+
+    def text_ends(s, rank):
+        text_out[s] = folded(line_partial[rank])
+        return text_out.at[s], text_in.at[s]
+
+    to_line(2, text_ends)
     spaced = jnp.concatenate(
         [grad.reshape(n_line, 1, rows, lanes), jnp.zeros((n_line, 1, rows, lanes), f32)], axis=1
     ).reshape(n_line * 2 * rows, lanes)
@@ -209,12 +215,12 @@
         spaced.astype(bf16), texts[...].reshape(n_line * 2 * rows, width),
         (((0,), (0,)), ((), ())), preferred_element_type=f32,
     ).reshape(n_plane, 2 * rows, width)
-    image_copies_2 = []
-    for s in range(n_plane - 1):
-        image_out[s] = folded(plane_partial[plane_peers[s][0], :rows, :])
-        copy = to_plane(2, s, image_out.at[s], image_in.at[s])
-        copy.start()
-        image_copies_2.append(copy)
+
+    def image_ends(s, rank):
+        image_out[s] = folded(plane_partial[rank, :rows, :])
+        return image_out.at[s], image_in.at[s]
+
+    to_plane(2, image_ends)
 
     def shares(lse, total, valid):
         share = lse[0:1] - mix_weight * (total[2:3] / total[1:2])
@@ -229,14 +235,8 @@
     line_loss_out[...] = jnp.where(line == 0, image_share, 0.0)
     line = lax.broadcasted_iota(jnp.int32, (8, text_lanes), 0)
     plane_loss_out[...] = jnp.where(line == 0, text_loss, 0.0)
-    line_copies_3 = [
-        to_line(3, s, line_loss_out, line_loss.at[s]) for s in range(n_line - 1)
-    ]
-    plane_copies_3 = [
-        to_plane(3, s, plane_loss_out, plane_loss.at[s]) for s in range(n_plane - 1)
-    ]
-    start(line_copies_3)
-    start(plane_copies_3)
+    to_line(3, lambda s, rank: (line_loss_out, line_loss.at[s]))
+    to_plane(3, lambda s, rank: (plane_loss_out, plane_loss.at[s]))
 
     def gathered(own, held, count):
         total = jnp.concatenate([own[:, :half], own[:, half:]], axis=0)
@@ -244,18 +244,18 @@
             total = total + held[s].astype(f32)
         return jnp.concatenate([total[:rows], total[rows:]], axis=1)
 
-    arrived(text_copies_2)
+    wait_all(line_recv, 2, line_spans[2])
     result[0] = gathered(line_partial[my_line], text_in, n_line - 1)
     results = [
         pltpu.make_async_copy(result.at[0], grad_text_ref, result_sem.at[0]),
         pltpu.make_async_copy(result.at[1], grad_image_ref, result_sem.at[1]),
     ]
     results[0].start()
-    arrived(image_copies_2)
+    wait_all(plane_recv, 2, plane_spans[2])
     result[1] = gathered(plane_partial[my_plane, :rows, :], image_in, n_plane - 1)
     results[1].start()
-    arrived(line_copies_3)
-    arrived(plane_copies_3)
+    wait_all(line_recv, 3, line_spans[3])
+    wait_all(plane_recv, 3, plane_spans[3])
     image_loss = line_loss_out[...]
     for s in range(n_line - 1):
         image_loss = image_loss + line_loss[s]
@@ -265,11 +265,9 @@
     total = jnp.sum(image_loss, keepdims=True) + jnp.sum(text_loss, keepdims=True)
     loss_ref[...] = total / (2.0 * rows * grp * blk)
 
-    for copy in (
-        image_copies + text_copies + image_copies_1 + text_copies_1
-        + image_copies_2 + text_copies_2 + line_copies_3 + plane_copies_3
-    ):
-        copy.wait_send()
+    for phase in range(4):
+        wait_all(line_send, phase, line_spans[phase])
+        wait_all(plane_send, phase, plane_spans[phase])
     for copy in results:
         copy.wait()
 
@@ -306,10 +304,10 @@
             pltpu.VMEM((8, lanes), f32),
             pltpu.VMEM((n_plane - 1, 8, text_lanes), f32),
             pltpu.VMEM((n_line - 1, 8, lanes), f32),
-            pltpu.SemaphoreType.DMA((4, n_plane - 1)),
-            pltpu.SemaphoreType.DMA((4, n_plane - 1)),
-            pltpu.SemaphoreType.DMA((4, n_line - 1)),
-            pltpu.SemaphoreType.DMA((4, n_line - 1)),
+            pltpu.SemaphoreType.DMA((4,)),
+            pltpu.SemaphoreType.DMA((4,)),
+            pltpu.SemaphoreType.DMA((4,)),
+            pltpu.SemaphoreType.DMA((4,)),
             pltpu.VMEM((4, rows, width), bf16),
             pltpu.SemaphoreType.DMA((4,)),
             pltpu.VMEM((2, rows, width), f32),

time: 25.4 us -> 24.7 us (0.972)
  Pallas kernels: 20.7 us -> 20 us
    pallas_call x1, Pallas kernels: 20.7 us -> 20 us  [local(): pl.pallas_call(functools.partial(kernel, grp, blk, fine, rows), out_shape...]
where the time goes in v4:
time: 24.7 us; the launch traced here: 24.3 us
  Pallas kernels  20 us (81%)
  between operations  2.34 us (9%)
  local copies, waits for them, and re-layouts  2 us (8%)
    pallas_call x1, Pallas kernels, local(): pl.pallas_call(functools.partial(kernel, grp, blk, fine, rows), out_shape...  20 us
    unnamed x4, local copies, waits for them, and re-layouts  2 us

profile of v4, /device:TPU:0, one launch (start us, length us, event | category | flops | bytes accessed | tf_op | source)
XLA Modules:
  0.0 24.3 jit_solution(8455956969795673622)
XLA Ops:
  0.6 20.0 %shard_map.67 = (f32[8,1024]{1,0:T(8,128)}, f32[8,1024]{1,0:T(8,128)}, f32[1,1]{1,0:T(1,128)}) custom-call(bf16[8,1024]{1,0:T(8,128)(2,1)} %image_ref.1, bf16[8,1024]{1,0:T(8,128)(2,1)} %text_ref.1, bf16[8,1024]{1,0:T(8,128)(2,1)} %mimage_ref.1, bf16[8,1024]{1,0:T(8,128)(2,1)} %mtext_ref.1), custom_call_target="tpu_custom_call" | custom-call | tf_op jit(solution)/shard_map/pallas_call | solution.py:283
  20.6 0.0 copy-start
  20.7 1.4 %copy.10 = f32[8,1024]{1,0:T(8,128)} copy(f32[8,1024]{1,0:T(8,128)} %get-tuple-element.12) | data formatting | bytes 65536
  22.0 0.0 copy-done
  22.0 0.6 %copy.11 = f32[8,1024]{1,0:T(8,128)} copy(f32[8,1024]{1,0:T(8,128)S(1)} %copy-done) | data formatting | bytes 65536
Async XLA Ops:
  20.6 1.4 %copy-start = (f32[8,1024]{1,0:T(8,128)S(1)}, f32[8,1024]{1,0:T(8,128)}, u32[]{:S(2)}) copy-start(f32[8,1024]{1,0:T(8,128)} %get-tuple-element.13) | copy-start | bytes 98308

commit v5 on v4

--- a/solution.py
+++ b/solution.py
@@ -269,6 +269,18 @@
         wait_all(line_send, phase, line_spans[phase])
         wait_all(plane_send, phase, plane_spans[phase])
     for copy in results:
+        copy.wait()
+
+
+def hand_over(image_in, text_in, loss_in, image_out, text_out, loss_out, sems):
+    copies = [
+        pltpu.make_async_copy(image_in, image_out, sems.at[0]),
+        pltpu.make_async_copy(text_in, text_out, sems.at[1]),
+        pltpu.make_async_copy(loss_in, loss_out, sems.at[2]),
+    ]
+    for copy in copies:
+        copy.start()
+    for copy in copies:
         copy.wait()
 
 
@@ -317,6 +329,15 @@
             collective_id=0, has_side_effects=True, vmem_limit_bytes=60 * 1024 * 1024
         ),
     )(image, text, mimage, mtext)
+    found = (grad_image, grad_text, loss)
+    grad_image, grad_text, loss = pl.pallas_call(
+        hand_over,
+        out_shape=tuple(jax.ShapeDtypeStruct(value.shape, value.dtype) for value in found),
+        in_specs=[in_hbm] * 3,
+        out_specs=(in_hbm,) * 3,
+        scratch_shapes=[pltpu.SemaphoreType.DMA((3,))],
+        compiler_params=pltpu.CompilerParams(vmem_limit_bytes=60 * 1024 * 1024),
+    )(*found)
     return grad_image, grad_text, loss.reshape(())
 
 

time: 24.7 us -> 24.7 us (level)
  Pallas kernels: 20 us -> 23.7 us
  local copies, waits for them, and re-layouts: 2 us -> 0 us
  between operations: 2.34 us -> 0.64 us
    pallas_call x0 -> x1, Pallas kernels: none -> 3.67 us  [local(): pl.pallas_call(hand_over, out_shape=tuple((jax.ShapeDtypeStruct(value.sha...]
    unnamed x4 -> x0, local copies, waits for them, and re-layouts: 2 us -> none
where the time goes in v5:
time: 24.7 us; the launch traced here: 24.3 us
  Pallas kernels  23.7 us (96%)
  between operations  0.64 us (3%)
    pallas_call x1, Pallas kernels, local(): pl.pallas_call(functools.partial(kernel, grp, blk, fine, rows), out_shape...  20 us
    pallas_call x1, Pallas kernels, local(): pl.pallas_call(hand_over, out_shape=tuple((jax.ShapeDtypeStruct(value.sha...  3.67 us

profile of v5, /device:TPU:0, one launch (start us, length us, event | category | flops | bytes accessed | tf_op | source)
XLA Modules:
  0.0 24.3 jit_solution(7637269752723270715)
XLA Ops:
  0.6 20.0 %shard_map.67 = (f32[8,1024]{1,0:T(8,128)}, f32[8,1024]{1,0:T(8,128)}, f32[1,1]{1,0:T(1,128)}) custom-call(bf16[8,1024]{1,0:T(8,128)(2,1)} %image_ref.1, bf16[8,1024]{1,0:T(8,128)(2,1)} %text_ref.1, bf16[8,1024]{1,0:T(8,128)(2,1)} %mimage_ref.1, bf16[8,1024]{1,0:T(8,128)(2,1)} %mtext_ref.1), custom_call_target="tpu_custom_call" | custom-call | tf_op jit(solution)/shard_map/pallas_call | solution.py:295
  20.6 3.7 %shard_map.68 = (f32[8,1024]{1,0:T(8,128)}, f32[8,1024]{1,0:T(8,128)}, f32[1,1]{1,0:T(1,128)}) custom-call(f32[8,1024]{1,0:T(8,128)} %get-tuple-element.9.image_in, f32[8,1024]{1,0:T(8,128)} %get-tuple-element.10.text_in, f32[1,1]{1,0:T(1,128)} %get-tuple-element.11.loss_in), custom_call_target="tpu_custom_call" | custom-call | tf_op jit(solution)/shard_map/pallas_call | solution.py:333

commit v6 on v5

--- a/solution.py
+++ b/solution.py
@@ -33,7 +33,7 @@
     grad_image_ref, grad_text_ref, loss_ref,
     images, texts, image_stats, text_stats, plane_partial, line_partial, image_out, text_out,
     image_in, text_in, plane_loss_out, line_loss_out, plane_loss, line_loss,
-    plane_send, plane_recv, line_send, line_recv, fetched, fetch_sem, result, result_sem,
+    plane_send, plane_recv, line_send, line_recv, fetched, fetch_sem, result, loss_held, result_sem,
 ):
     n_plane, n_line = fine * blk, grp // fine
     width = image_ref.shape[1]
@@ -249,6 +249,7 @@
     results = [
         pltpu.make_async_copy(result.at[0], grad_text_ref, result_sem.at[0]),
         pltpu.make_async_copy(result.at[1], grad_image_ref, result_sem.at[1]),
+        pltpu.make_async_copy(loss_held, loss_ref, result_sem.at[2]),
     ]
     results[0].start()
     wait_all(plane_recv, 2, plane_spans[2])
@@ -263,7 +264,8 @@
     for s in range(n_plane - 1):
         text_loss = text_loss + plane_loss[s]
     total = jnp.sum(image_loss, keepdims=True) + jnp.sum(text_loss, keepdims=True)
-    loss_ref[...] = total / (2.0 * rows * grp * blk)
+    loss_held[...] = total / (2.0 * rows * grp * blk)
+    results[2].start()
 
     for phase in range(4):
         wait_all(line_send, phase, line_spans[phase])
@@ -272,15 +274,21 @@
         copy.wait()
 
 
-def hand_over(image_in, text_in, loss_in, image_out, text_out, loss_out, sems):
-    copies = [
-        pltpu.make_async_copy(image_in, image_out, sems.at[0]),
-        pltpu.make_async_copy(text_in, text_out, sems.at[1]),
-        pltpu.make_async_copy(loss_in, loss_out, sems.at[2]),
-    ]
-    for copy in copies:
+def hand_over(*refs):
+    found, results, held = refs[:3], refs[3:6], refs[6:9]
+    in_sems, out_sems = refs[9:]
+    fetches = [
+        pltpu.make_async_copy(found[k], held[k], in_sems.at[k]) for k in range(3)
+    ]
+    writes = [
+        pltpu.make_async_copy(held[k], results[k], out_sems.at[k]) for k in range(3)
+    ]
+    for copy in fetches:
         copy.start()
-    for copy in copies:
+    for fetch, write in zip(fetches, writes):
+        fetch.wait()
+        write.start()
+    for copy in writes:
         copy.wait()
 
 
@@ -291,7 +299,6 @@
     lanes = n_plane * 2 * rows
     text_lanes = -(-n_line * rows // 128) * 128
     in_hbm = pl.BlockSpec(memory_space=pltpu.HBM)
-    in_vmem = pl.BlockSpec(memory_space=pltpu.VMEM)
     grad_image, grad_text, loss = pl.pallas_call(
         functools.partial(kernel, grp, blk, fine, rows),
         out_shape=(
@@ -300,7 +307,7 @@
             jax.ShapeDtypeStruct((1, 1), f32),
         ),
         in_specs=[in_hbm] * 4,
-        out_specs=(in_hbm, in_hbm, in_vmem),
+        out_specs=(in_hbm,) * 3,
         scratch_shapes=[
             pltpu.VMEM((n_plane, 2 * rows, width), bf16),
             pltpu.VMEM((n_line, 2 * rows, width), bf16),
@@ -323,7 +330,8 @@
             pltpu.VMEM((4, rows, width), bf16),
             pltpu.SemaphoreType.DMA((4,)),
             pltpu.VMEM((2, rows, width), f32),
-            pltpu.SemaphoreType.DMA((2,)),
+            pltpu.VMEM((1, 1), f32),
+            pltpu.SemaphoreType.DMA((3,)),
         ],
         compiler_params=pltpu.CompilerParams(
             collective_id=0, has_side_effects=True, vmem_limit_bytes=60 * 1024 * 1024
@@ -335,7 +343,11 @@
         out_shape=tuple(jax.ShapeDtypeStruct(value.shape, value.dtype) for value in found),
         in_specs=[in_hbm] * 3,
         out_specs=(in_hbm,) * 3,
-        scratch_shapes=[pltpu.SemaphoreType.DMA((3,))],
+        scratch_shapes=[
+            *(pltpu.VMEM(value.shape, value.dtype) for value in found),
+            pltpu.SemaphoreType.DMA((3,)),
+            pltpu.SemaphoreType.DMA((3,)),
+        ],
         compiler_params=pltpu.CompilerParams(vmem_limit_bytes=60 * 1024 * 1024),
     )(*found)
     return grad_image, grad_text, loss.reshape(())

time: 24.7 us -> 23 us (0.931)
  Pallas kernels: 23.7 us -> 22 us
    pallas_call x1, Pallas kernels: 3.67 us -> 2 us  [local(): pl.pallas_call(hand_over, out_shape=tuple((jax.ShapeDtypeStruct(value.sha...]
where the time goes in v6:
time: 23 us; the launch traced here: 22.6 us
  Pallas kernels  22 us (96%)
  between operations  0.64 us (3%)
    pallas_call x1, Pallas kernels, local(): pl.pallas_call(functools.partial(kernel, grp, blk, fine, rows), out_shape...  20 us
    pallas_call x1, Pallas kernels, local(): pl.pallas_call(hand_over, out_shape=tuple((jax.ShapeDtypeStruct(value.sha...  2 us

profile of v6, /device:TPU:0, one launch (start us, length us, event | category | flops | bytes accessed | tf_op | source)
XLA Modules:
  0.0 22.6 jit_solution(15936950258024076377)
XLA Ops:
  0.6 20.0 %shard_map.67 = (f32[8,1024]{1,0:T(8,128)}, f32[8,1024]{1,0:T(8,128)}, f32[1,1]{1,0:T(1,128)}) custom-call(bf16[8,1024]{1,0:T(8,128)(2,1)} %image_ref.1, bf16[8,1024]{1,0:T(8,128)(2,1)} %text_ref.1, bf16[8,1024]{1,0:T(8,128)(2,1)} %mimage_ref.1, bf16[8,1024]{1,0:T(8,128)(2,1)} %mtext_ref.1), custom_call_target="tpu_custom_call" | custom-call | tf_op jit(solution)/shard_map/pallas_call | solution.py:302
  20.6 2.0 %shard_map.68 = (f32[8,1024]{1,0:T(8,128)}, f32[8,1024]{1,0:T(8,128)}, f32[1,1]{1,0:T(1,128)}) custom-call(f32[8,1024]{1,0:T(8,128)} %get-tuple-element.9.refs_0_, f32[8,1024]{1,0:T(8,128)} %get-tuple-element.10.refs_1_, f32[1,1]{1,0:T(1,128)} %get-tuple-element.11.refs_2_), custom_call_target="tpu_custom_call" | custom-call | tf_op jit(solution)/shard_map/pallas_call | solution.py:341

commit v7 on v4

--- a/solution.py
+++ b/solution.py
@@ -33,7 +33,7 @@
     grad_image_ref, grad_text_ref, loss_ref,
     images, texts, image_stats, text_stats, plane_partial, line_partial, image_out, text_out,
     image_in, text_in, plane_loss_out, line_loss_out, plane_loss, line_loss,
-    plane_send, plane_recv, line_send, line_recv, fetched, fetch_sem, result, result_sem,
+    plane_send, plane_recv, line_send, line_recv, fetched, fetch_sem,
 ):
     n_plane, n_line = fine * blk, grp // fine
     width = image_ref.shape[1]
@@ -245,15 +245,9 @@
         return jnp.concatenate([total[:rows], total[rows:]], axis=1)
 
     wait_all(line_recv, 2, line_spans[2])
-    result[0] = gathered(line_partial[my_line], text_in, n_line - 1)
-    results = [
-        pltpu.make_async_copy(result.at[0], grad_text_ref, result_sem.at[0]),
-        pltpu.make_async_copy(result.at[1], grad_image_ref, result_sem.at[1]),
-    ]
-    results[0].start()
+    grad_text_ref[...] = gathered(line_partial[my_line], text_in, n_line - 1)
     wait_all(plane_recv, 2, plane_spans[2])
-    result[1] = gathered(plane_partial[my_plane, :rows, :], image_in, n_plane - 1)
-    results[1].start()
+    grad_image_ref[...] = gathered(plane_partial[my_plane, :rows, :], image_in, n_plane - 1)
     wait_all(line_recv, 3, line_spans[3])
     wait_all(plane_recv, 3, plane_spans[3])
     image_loss = line_loss_out[...]
@@ -262,13 +256,28 @@
     text_loss = plane_loss_out[...]
     for s in range(n_plane - 1):
         text_loss = text_loss + plane_loss[s]
-    total = jnp.sum(image_loss, keepdims=True) + jnp.sum(text_loss, keepdims=True)
-    loss_ref[...] = total / (2.0 * rows * grp * blk)
+    loss_ref[...] = sum(
+        value[:, first:first + 128]
+        for value in (image_loss, text_loss)
+        for first in range(0, value.shape[1], 128)
+    )
 
     for phase in range(4):
         wait_all(line_send, phase, line_spans[phase])
         wait_all(plane_send, phase, plane_spans[phase])
-    for copy in results:
+
+
+def hand_over(pairs, image_in, text_in, loss_in, image_out, text_out, loss_out, loss, sems):
+    copies = [
+        pltpu.make_async_copy(image_in, image_out, sems.at[0]),
+        pltpu.make_async_copy(text_in, text_out, sems.at[1]),
+        pltpu.make_async_copy(loss, loss_out, sems.at[2]),
+    ]
+    copies[0].start()
+    copies[1].start()
+    loss[...] = jnp.sum(loss_in[...], keepdims=True) / (2.0 * pairs)
+    copies[2].start()
+    for copy in copies:
         copy.wait()
 
 
@@ -278,6 +287,10 @@
     n_plane, n_line = fine * blk, grp // fine
     lanes = n_plane * 2 * rows
     text_lanes = -(-n_line * rows // 128) * 128
+    operands = [
+        pltpu.with_memory_space_constraint(value, pltpu.HBM)
+        for value in (image, text, mimage, mtext)
+    ]
     in_hbm = pl.BlockSpec(memory_space=pltpu.HBM)
     in_vmem = pl.BlockSpec(memory_space=pltpu.VMEM)
     grad_image, grad_text, loss = pl.pallas_call(
@@ -285,10 +298,10 @@
         out_shape=(
             jax.ShapeDtypeStruct((rows, width), f32),
             jax.ShapeDtypeStruct((rows, width), f32),
-            jax.ShapeDtypeStruct((1, 1), f32),
+            jax.ShapeDtypeStruct((8, 128), f32),
         ),
         in_specs=[in_hbm] * 4,
-        out_specs=(in_hbm, in_hbm, in_vmem),
+        out_specs=(in_vmem,) * 3,
         scratch_shapes=[
             pltpu.VMEM((n_plane, 2 * rows, width), bf16),
             pltpu.VMEM((n_line, 2 * rows, width), bf16),
@@ -310,13 +323,23 @@
             pltpu.SemaphoreType.DMA((4,)),
             pltpu.VMEM((4, rows, width), bf16),
             pltpu.SemaphoreType.DMA((4,)),
-            pltpu.VMEM((2, rows, width), f32),
-            pltpu.SemaphoreType.DMA((2,)),
         ],
         compiler_params=pltpu.CompilerParams(
-            collective_id=0, has_side_effects=True, vmem_limit_bytes=60 * 1024 * 1024
+            collective_id=0, has_side_effects=True, vmem_limit_bytes=32 * 1024 * 1024
         ),
-    )(image, text, mimage, mtext)
+    )(*operands)
+    grad_image, grad_text, loss = pl.pallas_call(
+        functools.partial(hand_over, rows * grp * blk),
+        out_shape=(
+            jax.ShapeDtypeStruct((rows, width), f32),
+            jax.ShapeDtypeStruct((rows, width), f32),
+            jax.ShapeDtypeStruct((1, 1), f32),
+        ),
+        in_specs=[in_vmem] * 3,
+        out_specs=(in_hbm,) * 3,
+        scratch_shapes=[pltpu.VMEM((1, 1), f32), pltpu.SemaphoreType.DMA((3,))],
+        compiler_params=pltpu.CompilerParams(vmem_limit_bytes=32 * 1024 * 1024),
+    )(grad_image, grad_text, loss)
     return grad_image, grad_text, loss.reshape(())
 
 

time: 24.7 us -> 20.9 us (0.85)
  local copies, waits for them, and re-layouts: 2 us -> 0 us
  between operations: 2.34 us -> 0.64 us
    unnamed x4 -> x0, local copies, waits for them, and re-layouts: 2 us -> none
    pallas_call x0 -> x1, Pallas kernels: none -> 0.66 us  [local(): pl.pallas_call(functools.partial(hand_over, rows * grp * blk), out_shape=...]
    pallas_call x1, Pallas kernels: 20 us -> 19.4 us  [local(): pl.pallas_call(functools.partial(kernel, grp, blk, fine, rows), out_shape...]
where the time goes in v7:
time: 20.9 us; the launch traced here: 20.7 us
  Pallas kernels  20 us (96%)
  between operations  0.64 us (3%)
    pallas_call x1, Pallas kernels, local(): pl.pallas_call(functools.partial(kernel, grp, blk, fine, rows), out_shape...  19.4 us
    pallas_call x1, Pallas kernels, local(): pl.pallas_call(functools.partial(hand_over, rows * grp * blk), out_shape=...  0.66 us

profile of v7, /device:TPU:0, one launch (start us, length us, event | category | flops | bytes accessed | tf_op | source)
XLA Modules:
  0.0 20.7 jit_solution(14143943130158839861)
XLA Ops:
  0.6 19.4 %shard_map.67 = (f32[8,1024]{1,0:T(8,128)S(1)}, f32[8,1024]{1,0:T(8,128)S(1)}, f32[8,128]{1,0:T(8,128)S(1)}) custom-call(bf16[8,1024]{1,0:T(8,128)(2,1)} %image_ref.1, bf16[8,1024]{1,0:T(8,128)(2,1)} %text_ref.1, bf16[8,1024]{1,0:T(8,128)(2,1)} %mimage_ref.1, bf16[8,1024]{1,0:T(8,128)(2,1)} %mtext_ref.1), custom_call_target="tpu_custom_call" | custom-call | tf_op jit(solution)/shard_map/pallas_call | solution.py:296
  20.0 0.7 %shard_map.68 = (f32[8,1024]{1,0:T(8,128)}, f32[8,1024]{1,0:T(8,128)}, f32[1,1]{1,0:T(1,128)}) custom-call(f32[8,1024]{1,0:T(8,128)S(1)} %get-tuple-element.9.image_in, f32[8,1024]{1,0:T(8,128)S(1)} %get-tuple-element.10.text_in, f32[8,128]{1,0:T(8,128)S(1)} %get-tuple-element.11.loss_in), custom_call_target="tpu_custom_call" | custom-call | tf_op jit(solution)/shard_map/pallas_call | solution.py:331

commit v8 on v7

--- a/solution.py
+++ b/solution.py
@@ -32,7 +32,7 @@
     image_ref, text_ref, mimage_ref, mtext_ref,
     grad_image_ref, grad_text_ref, loss_ref,
     images, texts, image_stats, text_stats, plane_partial, line_partial, image_out, text_out,
-    image_in, text_in, plane_loss_out, line_loss_out, plane_loss, line_loss,
+    image_in, text_in,
     plane_send, plane_recv, line_send, line_recv, fetched, fetch_sem,
 ):
     n_plane, n_line = fine * blk, grp // fine
@@ -81,9 +81,9 @@
 
     other_planes, other_lines = pl.ds(0, n_plane - 1), pl.ds(0, n_line - 1)
     plane_spans = [
-        images.at[other_planes], image_stats.at[other_planes], image_in, plane_loss,
+        images.at[other_planes], image_stats.at[other_planes], image_in,
     ]
-    line_spans = [texts.at[other_lines], text_stats.at[other_lines], text_in, line_loss]
+    line_spans = [texts.at[other_lines], text_stats.at[other_lines], text_in]
 
     barrier = pltpu.get_barrier_semaphore()
 
@@ -196,15 +196,44 @@
     grad = 0.5 * ((prob_row - target_row) + (prob_col - target_col))
     grad = jnp.where(online, grad, 0.0)
 
+    def shares(lse, total, valid):
+        share = lse[0:1] - mix_weight * (total[2:3] / total[1:2])
+        return jnp.where(valid, share, 0.0)
+
+    image_share = shares(image_lse, image_total, online[0:1])
+    image_share = image_share - jnp.where(
+        online[0:1], 2.0 * (1.0 - mix_weight) * image_total[3:4], 0.0
+    )
+    text_loss = shares(text_lse, text_total, in_text)
+    def narrow(share):
+        return sum(share[:, first:first + 128] for first in range(0, share.shape[1], 128))
+
+    image_share, text_loss = narrow(image_share), narrow(text_loss)
+
+    def rider(share):
+        head = share.astype(bf16).astype(f32)
+        middle = (share - head).astype(bf16).astype(f32)
+        tail = share - head - middle
+        line = lax.broadcasted_iota(jnp.int32, (2 * rows, 128), 0)
+        return jnp.where(
+            line == 0, head, jnp.where(line == 1, middle, jnp.where(line == 2, tail, 0.0))
+        )
+
+    image_rider, text_rider = rider(image_share), rider(text_loss)
+
     def folded(value):
-        return jnp.concatenate([value[:, :half], value[:, half:]], axis=0).astype(bf16)
+        return jnp.concatenate([value[:, :half], value[:, half:]], axis=0)
+
+    def put(target, value, extra):
+        target[:, :half] = folded(value).astype(bf16)
+        target[:, half:] = extra.astype(bf16)
 
     line_partial[...] = jnp.dot(
         grad.astype(bf16), images[...].reshape(lanes, width), preferred_element_type=f32
     ).reshape(n_line, rows, width)
 
     def text_ends(s, rank):
-        text_out[s] = folded(line_partial[rank])
+        put(text_out.at[s], line_partial[rank], image_rider)
         return text_out.at[s], text_in.at[s]
 
     to_line(2, text_ends)
@@ -217,52 +246,29 @@
     ).reshape(n_plane, 2 * rows, width)
 
     def image_ends(s, rank):
-        image_out[s] = folded(plane_partial[rank, :rows, :])
+        put(image_out.at[s], plane_partial[rank, :rows, :], text_rider)
         return image_out.at[s], image_in.at[s]
 
     to_plane(2, image_ends)
 
-    def shares(lse, total, valid):
-        share = lse[0:1] - mix_weight * (total[2:3] / total[1:2])
-        return jnp.where(valid, share, 0.0)
-
-    image_share = shares(image_lse, image_total, online[0:1])
-    image_share = image_share - jnp.where(
-        online[0:1], 2.0 * (1.0 - mix_weight) * image_total[3:4], 0.0
-    )
-    text_loss = shares(text_lse, text_total, in_text)
-    line = lax.broadcasted_iota(jnp.int32, (8, lanes), 0)
-    line_loss_out[...] = jnp.where(line == 0, image_share, 0.0)
-    line = lax.broadcasted_iota(jnp.int32, (8, text_lanes), 0)
-    plane_loss_out[...] = jnp.where(line == 0, text_loss, 0.0)
-    to_line(3, lambda s, rank: (line_loss_out, line_loss.at[s]))
-    to_plane(3, lambda s, rank: (plane_loss_out, plane_loss.at[s]))
-
-    def gathered(own, held, count):
-        total = jnp.concatenate([own[:, :half], own[:, half:]], axis=0)
+    def gathered(own, held, count, extra):
+        total, share = folded(own), extra
         for s in range(count):
-            total = total + held[s].astype(f32)
-        return jnp.concatenate([total[:rows], total[rows:]], axis=1)
+            total = total + held[s, :, :half].astype(f32)
+            share = share + held[s, :, half:].astype(f32)
+        return jnp.concatenate([total[:rows], total[rows:]], axis=1), share
 
     wait_all(line_recv, 2, line_spans[2])
-    grad_text_ref[...] = gathered(line_partial[my_line], text_in, n_line - 1)
+    grad_text_ref[...], image_loss = gathered(
+        line_partial[my_line], text_in, n_line - 1, image_rider
+    )
     wait_all(plane_recv, 2, plane_spans[2])
-    grad_image_ref[...] = gathered(plane_partial[my_plane, :rows, :], image_in, n_plane - 1)
-    wait_all(line_recv, 3, line_spans[3])
-    wait_all(plane_recv, 3, plane_spans[3])
-    image_loss = line_loss_out[...]
-    for s in range(n_line - 1):
-        image_loss = image_loss + line_loss[s]
-    text_loss = plane_loss_out[...]
-    for s in range(n_plane - 1):
-        text_loss = text_loss + plane_loss[s]
-    loss_ref[...] = sum(
-        value[:, first:first + 128]
-        for value in (image_loss, text_loss)
-        for first in range(0, value.shape[1], 128)
-    )
-
-    for phase in range(4):
+    grad_image_ref[...], text_loss = gathered(
+        plane_partial[my_plane, :rows, :], image_in, n_plane - 1, text_rider
+    )
+    loss_ref[...] = image_loss + text_loss
+
+    for phase in range(3):
         wait_all(line_send, phase, line_spans[phase])
         wait_all(plane_send, phase, plane_spans[phase])
 
@@ -298,7 +304,7 @@
         out_shape=(
             jax.ShapeDtypeStruct((rows, width), f32),
             jax.ShapeDtypeStruct((rows, width), f32),
-            jax.ShapeDtypeStruct((8, 128), f32),
+            jax.ShapeDtypeStruct((2 * rows, 128), f32),
         ),
         in_specs=[in_hbm] * 4,
         out_specs=(in_vmem,) * 3,
@@ -309,18 +315,14 @@
             pltpu.VMEM((n_line, 16, text_lanes), f32),
             pltpu.VMEM((n_plane, 2 * rows, width), f32),
             pltpu.VMEM((n_line, rows, width), f32),
-            pltpu.VMEM((n_plane - 1, 2 * rows, width // 2), bf16),
-            pltpu.VMEM((n_line - 1, 2 * rows, width // 2), bf16),
-            pltpu.VMEM((n_plane - 1, 2 * rows, width // 2), bf16),
-            pltpu.VMEM((n_line - 1, 2 * rows, width // 2), bf16),
-            pltpu.VMEM((8, text_lanes), f32),
-            pltpu.VMEM((8, lanes), f32),
-            pltpu.VMEM((n_plane - 1, 8, text_lanes), f32),
-            pltpu.VMEM((n_line - 1, 8, lanes), f32),
-            pltpu.SemaphoreType.DMA((4,)),
-            pltpu.SemaphoreType.DMA((4,)),
-            pltpu.SemaphoreType.DMA((4,)),
-            pltpu.SemaphoreType.DMA((4,)),
+            pltpu.VMEM((n_plane - 1, 2 * rows, width // 2 + 128), bf16),
+            pltpu.VMEM((n_line - 1, 2 * rows, width // 2 + 128), bf16),
+            pltpu.VMEM((n_plane - 1, 2 * rows, width // 2 + 128), bf16),
+            pltpu.VMEM((n_line - 1, 2 * rows, width // 2 + 128), bf16),
+            pltpu.SemaphoreType.DMA((3,)),
+            pltpu.SemaphoreType.DMA((3,)),
+            pltpu.SemaphoreType.DMA((3,)),
+            pltpu.SemaphoreType.DMA((3,)),
             pltpu.VMEM((4, rows, width), bf16),
             pltpu.SemaphoreType.DMA((4,)),
         ],

time: 20.9 us -> 20.3 us (0.971)
  Pallas kernels: 20 us -> 19.5 us
    pallas_call x1, Pallas kernels: 19.4 us -> 18.8 us  [local(): pl.pallas_call(functools.partial(kernel, grp, blk, fine, rows), out_shape...]
where the time goes in v8:
time: 20.3 us; the launch traced here: 20.1 us
  Pallas kernels  19.5 us (96%)
  between operations  0.64 us (3%)
    pallas_call x1, Pallas kernels, local(): pl.pallas_call(functools.partial(kernel, grp, blk, fine, rows), out_shape...  18.8 us
    pallas_call x1, Pallas kernels, local(): pl.pallas_call(functools.partial(hand_over, rows * grp * blk), out_shape=...  0.66 us

profile of v8, /device:TPU:0, one launch (start us, length us, event | category | flops | bytes accessed | tf_op | source)
XLA Modules:
  0.0 20.1 jit_solution(8603912959101946875)
XLA Ops:
  0.6 18.8 %shard_map.67 = (f32[8,1024]{1,0:T(8,128)S(1)}, f32[8,1024]{1,0:T(8,128)S(1)}, f32[16,128]{1,0:T(8,128)S(1)}) custom-call(bf16[8,1024]{1,0:T(8,128)(2,1)} %image_ref.1, bf16[8,1024]{1,0:T(8,128)(2,1)} %text_ref.1, bf16[8,1024]{1,0:T(8,128)(2,1)} %mimage_ref.1, bf16[8,1024]{1,0:T(8,128)(2,1)} %mtext_ref.1), custom_call_target="tpu_custom_call" | custom-call | tf_op jit(solution)/shard_map/pallas_call | solution.py:302
  19.5 0.7 %shard_map.68 = (f32[8,1024]{1,0:T(8,128)}, f32[8,1024]{1,0:T(8,128)}, f32[1,1]{1,0:T(1,128)}) custom-call(f32[8,1024]{1,0:T(8,128)S(1)} %get-tuple-element.9.image_in, f32[8,1024]{1,0:T(8,128)S(1)} %get-tuple-element.10.text_in, f32[16,128]{1,0:T(8,128)S(1)} %get-tuple-element.11.loss_in), custom_call_target="tpu_custom_call" | custom-call | tf_op jit(solution)/shard_map/pallas_call | solution.py:333

commit v9 on v8

--- a/solution.py
+++ b/solution.py
@@ -159,19 +159,21 @@
 
     def message(top_on, sum_on, top_mom, sum_mom, cross, diag):
         line = lax.broadcasted_iota(jnp.int32, (8, top_on.shape[1]), 0)
-        tops = jnp.where(line == 0, top_on, jnp.where((line == 1) | (line == 2), top_mom, 0.0))
-        sums = jnp.where(line == 0, sum_on, jnp.where(line == 1, sum_mom, 1.0))
-        sums = jnp.where(line == 2, cross, jnp.where(line == 3, diag, sums))
-        return jnp.concatenate([tops, sums], axis=0)
+        tile = diag
+        for row, part in enumerate((top_on, top_mom, sum_on, sum_mom, cross)):
+            tile = jnp.where(line == row, part, tile)
+        return tile
 
     def joined(held, count):
-        top = held[0, :8]
-        for k in range(1, count):
-            top = jnp.maximum(top, held[k, :8])
-        total = held[0, 8:] * jnp.exp(held[0, :8] - top)
-        for k in range(1, count):
-            total = total + held[k, 8:] * jnp.exp(held[k, :8] - top)
-        return top + jnp.log(total), total
+        line = lax.broadcasted_iota(jnp.int32, held.shape[1:], 0)
+        tiles = [held[k] for k in range(count)]
+        tops = [
+            jnp.where(line == 2, tile[0:1], jnp.where((line == 3) | (line == 4), tile[1:2], 0.0))
+            for tile in tiles
+        ]
+        top = functools.reduce(jnp.maximum, tops)
+        total = sum(tile * jnp.exp(mine - top) for tile, mine in zip(tiles, tops))
+        return top[2:4] + jnp.log(total[2:4]), total
 
     text_part = [to_lanes(column) for column in stats(masked_on, masked_mom, 1)]
     in_text = lax.broadcasted_iota(jnp.int32, (1, text_lanes), 1) < text_rows
@@ -197,14 +199,15 @@
     grad = jnp.where(online, grad, 0.0)
 
     def shares(lse, total, valid):
-        share = lse[0:1] - mix_weight * (total[2:3] / total[1:2])
+        share = lse[0:1] - mix_weight * (total[4:5] / total[3:4])
         return jnp.where(valid, share, 0.0)
 
     image_share = shares(image_lse, image_total, online[0:1])
     image_share = image_share - jnp.where(
-        online[0:1], 2.0 * (1.0 - mix_weight) * image_total[3:4], 0.0
+        online[0:1], 2.0 * (1.0 - mix_weight) * image_total[5:6], 0.0
     )
     text_loss = shares(text_lse, text_total, in_text)
+
     def narrow(share):
         return sum(share[:, first:first + 128] for first in range(0, share.shape[1], 128))
 
@@ -311,8 +314,8 @@
         scratch_shapes=[
             pltpu.VMEM((n_plane, 2 * rows, width), bf16),
             pltpu.VMEM((n_line, 2 * rows, width), bf16),
-            pltpu.VMEM((n_plane, 16, lanes), f32),
-            pltpu.VMEM((n_line, 16, text_lanes), f32),
+            pltpu.VMEM((n_plane, 8, lanes), f32),
+            pltpu.VMEM((n_line, 8, text_lanes), f32),
             pltpu.VMEM((n_plane, 2 * rows, width), f32),
             pltpu.VMEM((n_line, rows, width), f32),
             pltpu.VMEM((n_plane - 1, 2 * rows, width // 2 + 128), bf16),

time: 20.3 us -> 20.3 us (level)
  no operation moved by 1% of the time
where the time goes in v9:
time: 20.3 us; the launch traced here: 20.1 us
  Pallas kernels  19.4 us (96%)
  between operations  0.64 us (3%)
    pallas_call x1, Pallas kernels, local(): pl.pallas_call(functools.partial(kernel, grp, blk, fine, rows), out_shape...  18.8 us
    pallas_call x1, Pallas kernels, local(): pl.pallas_call(functools.partial(hand_over, rows * grp * blk), out_shape=...  0.66 us

profile of v9, /device:TPU:0, one launch (start us, length us, event | category | flops | bytes accessed | tf_op | source)
XLA Modules:
  0.0 20.1 jit_solution(3149992909183322237)
XLA Ops:
  0.6 18.8 %shard_map.67 = (f32[8,1024]{1,0:T(8,128)S(1)}, f32[8,1024]{1,0:T(8,128)S(1)}, f32[16,128]{1,0:T(8,128)S(1)}) custom-call(bf16[8,1024]{1,0:T(8,128)(2,1)} %image_ref.1, bf16[8,1024]{1,0:T(8,128)(2,1)} %text_ref.1, bf16[8,1024]{1,0:T(8,128)(2,1)} %mimage_ref.1, bf16[8,1024]{1,0:T(8,128)(2,1)} %mtext_ref.1), custom_call_target="tpu_custom_call" | custom-call | tf_op jit(solution)/shard_map/pallas_call | solution.py:305
  19.4 0.7 %shard_map.68 = (f32[8,1024]{1,0:T(8,128)}, f32[8,1024]{1,0:T(8,128)}, f32[1,1]{1,0:T(1,128)}) custom-call(f32[8,1024]{1,0:T(8,128)S(1)} %get-tuple-element.9.image_in, f32[8,1024]{1,0:T(8,128)S(1)} %get-tuple-element.10.text_in, f32[16,128]{1,0:T(8,128)S(1)} %get-tuple-element.11.loss_in), custom_call_target="tpu_custom_call" | custom-call | tf_op jit(solution)/shard_map/pallas_call | solution.py:336

commit v10 on v9

--- a/solution.py
+++ b/solution.py
@@ -33,7 +33,7 @@
     grad_image_ref, grad_text_ref, loss_ref,
     images, texts, image_stats, text_stats, plane_partial, line_partial, image_out, text_out,
     image_in, text_in,
-    plane_send, plane_recv, line_send, line_recv, fetched, fetch_sem,
+    plane_send, plane_recv, line_send, line_recv, fetched, fetch_sem, chip_recv,
 ):
     n_plane, n_line = fine * blk, grp // fine
     width = image_ref.shape[1]
@@ -115,7 +115,23 @@
     pl.semaphore_wait(barrier, n_plane + n_line - 2)
 
     to_line(0, lambda s, rank: (texts.at[my_line], texts.at[my_line]))
-    to_plane(0, lambda s, rank: (images.at[my_plane], images.at[my_plane]))
+    chips = n_plane // 2
+    core = lax.rem(my_plane, 2)
+    sibling = my_plane + 1 - 2 * core
+
+    def peer_at(rank):
+        return (my_line * fine + lax.div(rank, blk), lax.rem(rank, blk))
+
+    def pass_on(rank, peer, sem):
+        return pltpu.make_async_remote_copy(
+            src_ref=images.at[rank], dst_ref=images.at[rank],
+            send_sem=plane_send.at[0], recv_sem=sem,
+            device_id=peer_at(peer), device_id_type=MESH,
+        )
+
+    for d in range(1, chips):
+        pass_on(my_plane, lax.rem(my_plane + 2 * d, n_plane), chip_recv.at[d - 1]).start()
+    pass_on(my_plane, sibling, plane_recv.at[0]).start()
 
     shape = (text_rows, lanes)
     text_slot, text_sub = split_index(lax.broadcasted_iota(jnp.int32, shape, 0), rows)
@@ -135,8 +151,12 @@
     def to_column(row):
         return jnp.sum(jnp.where(eye, row, 0.0), axis=1, keepdims=True)
 
+    for d in range(1, chips):
+        source = lax.rem(my_plane + n_plane - 2 * d, n_plane)
+        wait_all(chip_recv, d - 1, images.at[source])
+        pass_on(source, sibling, plane_recv.at[0]).start()
     wait_all(line_recv, 0, line_spans[0])
-    wait_all(plane_recv, 0, plane_spans[0])
+    wait_all(plane_recv, 0, images.at[pl.ds(0, chips)])
     scores = lax.dot_general(
         texts[...].reshape(n_line * 2 * rows, width), images[...].reshape(lanes, width),
         (((1,), (1,)), ((), ())), preferred_element_type=f32,
@@ -328,6 +348,7 @@
             pltpu.SemaphoreType.DMA((3,)),
             pltpu.VMEM((4, rows, width), bf16),
             pltpu.SemaphoreType.DMA((4,)),
+            pltpu.SemaphoreType.DMA((max(n_plane // 2 - 1, 1),)),
         ],
         compiler_params=pltpu.CompilerParams(
             collective_id=0, has_side_effects=True, vmem_limit_bytes=32 * 1024 * 1024

time: 20.3 us -> 20.3 us (level)
  no operation moved by 1% of the time
where the time goes in v10:
time: 20.3 us; the launch traced here: 20.1 us
  Pallas kernels  19.5 us (96%)
  between operations  0.64 us (3%)
    pallas_call x1, Pallas kernels, local(): pl.pallas_call(functools.partial(kernel, grp, blk, fine, rows), out_shape...  18.8 us
    pallas_call x1, Pallas kernels, local(): pl.pallas_call(functools.partial(hand_over, rows * grp * blk), out_shape=...  0.66 us

profile of v10, /device:TPU:0, one launch (start us, length us, event | category | flops | bytes accessed | tf_op | source)
XLA Modules:
  0.0 20.1 jit_solution(5784212794986627883)
XLA Ops:
  0.6 18.8 %shard_map.67 = (f32[8,1024]{1,0:T(8,128)S(1)}, f32[8,1024]{1,0:T(8,128)S(1)}, f32[16,128]{1,0:T(8,128)S(1)}) custom-call(bf16[8,1024]{1,0:T(8,128)(2,1)} %image_ref.1, bf16[8,1024]{1,0:T(8,128)(2,1)} %text_ref.1, bf16[8,1024]{1,0:T(8,128)(2,1)} %mimage_ref.1, bf16[8,1024]{1,0:T(8,128)(2,1)} %mtext_ref.1), custom_call_target="tpu_custom_call" | custom-call | tf_op jit(solution)/shard_map/pallas_call | solution.py:325
  19.4 0.7 %shard_map.68 = (f32[8,1024]{1,0:T(8,128)}, f32[8,1024]{1,0:T(8,128)}, f32[1,1]{1,0:T(1,128)}) custom-call(f32[8,1024]{1,0:T(8,128)S(1)} %get-tuple-element.9.image_in, f32[8,1024]{1,0:T(8,128)S(1)} %get-tuple-element.10.text_in, f32[16,128]{1,0:T(8,128)S(1)} %get-tuple-element.11.loss_in), custom_call_target="tpu_custom_call" | custom-call | tf_op jit(solution)/shard_map/pallas_call | solution.py:357

commit v11 on v9

--- a/solution.py
+++ b/solution.py
@@ -108,13 +108,14 @@
     def pair(first, second):
         return jnp.concatenate([first.astype(f32), second.astype(f32)], axis=0).astype(bf16)
 
-    for copy in fetches:
-        copy.wait()
+    fetches[0].wait()
+    fetches[1].wait()
     texts[my_line] = pair(fetched[0], fetched[1])
+    pl.semaphore_wait(barrier, n_plane + n_line - 2)
+    to_line(0, lambda s, rank: (texts.at[my_line], texts.at[my_line]))
+    fetches[2].wait()
+    fetches[3].wait()
     images[my_plane] = pair(fetched[2], fetched[3])
-    pl.semaphore_wait(barrier, n_plane + n_line - 2)
-
-    to_line(0, lambda s, rank: (texts.at[my_line], texts.at[my_line]))
     to_plane(0, lambda s, rank: (images.at[my_plane], images.at[my_plane]))
 
     shape = (text_rows, lanes)

time: 20.3 us -> 20.3 us (level)
  no operation moved by 1% of the time
where the time goes in v11:
time: 20.3 us; the launch traced here: 20.1 us
  Pallas kernels  19.4 us (96%)
  between operations  0.64 us (3%)
    pallas_call x1, Pallas kernels, local(): pl.pallas_call(functools.partial(kernel, grp, blk, fine, rows), out_shape...  18.8 us
    pallas_call x1, Pallas kernels, local(): pl.pallas_call(functools.partial(hand_over, rows * grp * blk), out_shape=...  0.66 us

profile of v11, /device:TPU:0, one launch (start us, length us, event | category | flops | bytes accessed | tf_op | source)
XLA Modules:
  0.0 20.1 jit_solution(17185715052817348795)
XLA Ops:
  0.6 18.8 %shard_map.67 = (f32[8,1024]{1,0:T(8,128)S(1)}, f32[8,1024]{1,0:T(8,128)S(1)}, f32[16,128]{1,0:T(8,128)S(1)}) custom-call(bf16[8,1024]{1,0:T(8,128)(2,1)} %image_ref.1, bf16[8,1024]{1,0:T(8,128)(2,1)} %text_ref.1, bf16[8,1024]{1,0:T(8,128)(2,1)} %mimage_ref.1, bf16[8,1024]{1,0:T(8,128)(2,1)} %mtext_ref.1), custom_call_target="tpu_custom_call" | custom-call | tf_op jit(solution)/shard_map/pallas_call | solution.py:306
  19.4 0.7 %shard_map.68 = (f32[8,1024]{1,0:T(8,128)}, f32[8,1024]{1,0:T(8,128)}, f32[1,1]{1,0:T(1,128)}) custom-call(f32[8,1024]{1,0:T(8,128)S(1)} %get-tuple-element.9.image_in, f32[8,1024]{1,0:T(8,128)S(1)} %get-tuple-element.10.text_in, f32[16,128]{1,0:T(8,128)S(1)} %get-tuple-element.11.loss_in), custom_call_target="tpu_custom_call" | custom-call | tf_op jit(solution)/shard_map/pallas_call | solution.py:337

commit v12 on v11

--- a/solution.py
+++ b/solution.py
@@ -262,6 +262,9 @@
             share = share + held[s, :, half:].astype(f32)
         return jnp.concatenate([total[:rows], total[rows:]], axis=1), share
 
+    for phase in range(2):
+        wait_all(line_send, phase, line_spans[phase])
+        wait_all(plane_send, phase, plane_spans[phase])
     wait_all(line_recv, 2, line_spans[2])
     grad_text_ref[...], image_loss = gathered(
         line_partial[my_line], text_in, n_line - 1, image_rider
@@ -272,9 +275,8 @@
     )
     loss_ref[...] = image_loss + text_loss
 
-    for phase in range(3):
-        wait_all(line_send, phase, line_spans[phase])
-        wait_all(plane_send, phase, plane_spans[phase])
+    wait_all(line_send, 2, line_spans[2])
+    wait_all(plane_send, 2, plane_spans[2])
 
 
 def hand_over(pairs, image_in, text_in, loss_in, image_out, text_out, loss_out, loss, sems):

time: 20.3 us -> 20.3 us (level)
  no operation moved by 1% of the time
where the time goes in v12:
time: 20.3 us; the launch traced here: 20.1 us
  Pallas kernels  19.4 us (96%)
  between operations  0.64 us (3%)
    pallas_call x1, Pallas kernels, local(): pl.pallas_call(functools.partial(kernel, grp, blk, fine, rows), out_shape...  18.8 us
    pallas_call x1, Pallas kernels, local(): pl.pallas_call(functools.partial(hand_over, rows * grp * blk), out_shape=...  0.66 us

profile of v12, /device:TPU:0, one launch (start us, length us, event | category | flops | bytes accessed | tf_op | source)
XLA Modules:
  0.0 20.1 jit_solution(15578581522308358957)
XLA Ops:
  0.6 18.8 %shard_map.67 = (f32[8,1024]{1,0:T(8,128)S(1)}, f32[8,1024]{1,0:T(8,128)S(1)}, f32[16,128]{1,0:T(8,128)S(1)}) custom-call(bf16[8,1024]{1,0:T(8,128)(2,1)} %image_ref.1, bf16[8,1024]{1,0:T(8,128)(2,1)} %text_ref.1, bf16[8,1024]{1,0:T(8,128)(2,1)} %mimage_ref.1, bf16[8,1024]{1,0:T(8,128)(2,1)} %mtext_ref.1), custom_call_target="tpu_custom_call" | custom-call | tf_op jit(solution)/shard_map/pallas_call | solution.py:308
  19.4 0.7 %shard_map.68 = (f32[8,1024]{1,0:T(8,128)}, f32[8,1024]{1,0:T(8,128)}, f32[1,1]{1,0:T(1,128)}) custom-call(f32[8,1024]{1,0:T(8,128)S(1)} %get-tuple-element.9.image_in, f32[8,1024]{1,0:T(8,128)S(1)} %get-tuple-element.10.text_in, f32[16,128]{1,0:T(8,128)S(1)} %get-tuple-element.11.loss_in), custom_call_target="tpu_custom_call" | custom-call | tf_op jit(solution)/shard_map/pallas_call | solution.py:339

commit v13 on v11

--- a/solution.py
+++ b/solution.py
@@ -66,7 +66,7 @@
             ).start()
             return carry
 
-        lax.fori_loop(0, count - 1, step, 0)
+        lax.fori_loop(0, count - 1, step, 0, unroll=count <= 4)
 
     def wait_all(sem, phase, span):
         pltpu.make_async_copy(span, span, sem.at[phase]).wait()
@@ -94,7 +94,7 @@
             )
             return carry
 
-        lax.fori_loop(0, count - 1, step, 0)
+        lax.fori_loop(0, count - 1, step, 0, unroll=count <= 4)
 
     greet(line_peer, n_line)
     greet(plane_peer, n_plane)

time: 20.3 us -> 20.3 us (level)
  no operation moved by 1% of the time
where the time goes in v13:
time: 20.3 us; the launch traced here: 20 us
  Pallas kernels  19.4 us (96%)
  between operations  0.64 us (3%)
    pallas_call x1, Pallas kernels, local(): pl.pallas_call(functools.partial(kernel, grp, blk, fine, rows), out_shape...  18.7 us
    pallas_call x1, Pallas kernels, local(): pl.pallas_call(functools.partial(hand_over, rows * grp * blk), out_shape=...  0.66 us

profile of v13, /device:TPU:0, one launch (start us, length us, event | category | flops | bytes accessed | tf_op | source)
XLA Modules:
  0.0 20.0 jit_solution(17130768638352476178)
XLA Ops:
  0.6 18.7 %shard_map.67 = (f32[8,1024]{1,0:T(8,128)S(1)}, f32[8,1024]{1,0:T(8,128)S(1)}, f32[16,128]{1,0:T(8,128)S(1)}) custom-call(bf16[8,1024]{1,0:T(8,128)(2,1)} %image_ref.1, bf16[8,1024]{1,0:T(8,128)(2,1)} %text_ref.1, bf16[8,1024]{1,0:T(8,128)(2,1)} %mimage_ref.1, bf16[8,1024]{1,0:T(8,128)(2,1)} %mtext_ref.1), custom_call_target="tpu_custom_call" | custom-call | tf_op jit(solution)/shard_map/pallas_call | solution.py:306
  19.4 0.7 %shard_map.68 = (f32[8,1024]{1,0:T(8,128)}, f32[8,1024]{1,0:T(8,128)}, f32[1,1]{1,0:T(1,128)}) custom-call(f32[8,1024]{1,0:T(8,128)S(1)} %get-tuple-element.9.image_in, f32[8,1024]{1,0:T(8,128)S(1)} %get-tuple-element.10.text_in, f32[16,128]{1,0:T(8,128)S(1)} %get-tuple-element.11.loss_in), custom_call_target="tpu_custom_call" | custom-call | tf_op jit(solution)/shard_map/pallas_call | solution.py:337
